TPU v7x, 32 devices: a whole 2x2x4 slice. The times are simulated.
32 devices in a mesh: dp: 16 (over z, y, core), tensor: 2 (over x).
Axes of the slice: x: 2, y: 2, z: 4, core: 2. Of those that a mesh axis runs over, the one named last changes fastest.
Arguments:
- tokens: bfloat16 [16, 1024, 1024], P('dp', 'tensor'), may hold values from -6 to 6
- segment_ids: int32 [16, 1024], P('dp'), may hold values from 0 to 2, as said below
- norm_gains: float32 [2, 1024], replicated, may hold values from 0.25 to 1.75
- w_mixer_in: bfloat16 [1024, 4, 8, 128], P('dp', None, 'tensor'), may hold values from -0.1875 to 0.1875
- w_rates: bfloat16 [1024, 2, 8], P('dp', None, 'tensor'), may hold values from -0.1875 to 0.1875
- conv_weight: bfloat16 [3, 4, 8, 128], P(None, None, 'tensor', 'dp'), may hold values from -3 to 3
- a_log: float32 [8], replicated, may hold values from -7 to -3
- out_gain: float32 [128], replicated, may hold values from 0.25 to 1.75
- w_output: bfloat16 [1024, 1024], P('tensor', 'dp'), may hold values from -0.25 to 0.25
- w_gate_up: bfloat16 [1024, 2, 2816], P('dp', None, 'tensor'), may hold values from -0.1875 to 0.1875
- w_down: bfloat16 [2816, 1024], P('tensor', 'dp'), may hold values from -0.21875 to 0.21875
- cotangent: bfloat16 [16, 1024, 1024], P('dp', 'tensor'), may hold values from -6 to 6
Outputs:
- out_tokens: bfloat16 [16, 1024, 1024], P('dp', 'tensor')
- grad_tokens: bfloat16 [16, 1024, 1024], P('dp', 'tensor')
- grad_norm_gains: float32 [2, 1024], replicated
- grad_w_mixer_in: float32 [1024, 4, 8, 128], P('dp', None, 'tensor')
- grad_w_rates: float32 [1024, 2, 8], P('dp', None, 'tensor')
- grad_conv_weight: float32 [3, 4, 8, 128], P(None, None, 'tensor', 'dp')
- grad_a_log: float32 [8], replicated
- grad_out_gain: float32 [128], replicated
- grad_w_output: float32 [1024, 1024], P('tensor', 'dp')
- grad_w_gate_up: float32 [1024, 2, 2816], P('dp', None, 'tensor')
- grad_w_down: float32 [2816, 1024], P('tensor', 'dp')
Inputs may be any that keep to these rules, and one draw needn't show every extreme that they name: `segment_ids`: each sequence holds exactly three documents, numbered 0, 1 and 2 in order along it, each of 200 tokens or more; document numbers never fall along a sequence.
All inputs are finite; a program needn't handle non-finite values.
Results may differ from a plain program's by a relative error of at most 0.022.
Values may be sent and summed in bfloat16 or wider, within the bound.
No kernel may reach another device: no remote copies, remote signals or barrier semaphores. Data moves between devices by JAX's collectives and lax.ppermute only.
A program may use at most 256 MiB of HBM per device.

v0:
```python
import jax
import jax.numpy as jnp
from jax import lax
from jax.sharding import PartitionSpec as P

SPAN = 64


highest = lax.Precision.HIGHEST
norm_eps = 1e-05
unit_eps = 1e-06


def rms_norm(values, scales):
    return values * lax.rsqrt(jnp.mean(values * values, axis=-1, keepdims=True) + norm_eps) * scales


def first_norm(values, gains):
    return rms_norm(values, gains[0])


def second_norm(values, gains):
    return rms_norm(values, gains[1])


def swish_product(gate_up):
    return jax.nn.silu(gate_up[:, 0]) * gate_up[:, 1]


def contract_last(operand, other):
    return lax.dot_general(
        operand, other, (((1,), (1,)), ((), ())), preferred_element_type=jnp.float32
    )


def contract_first(operand, other):
    return lax.dot_general(
        operand, other, (((0,), (0,)), ((), ())), preferred_element_type=jnp.float32
    )


def short_conv(signal, weight, segment):
    length = signal.shape[0]
    tap_count = weight.shape[0]
    result = jnp.zeros_like(signal)
    for offset in range(tap_count):
        shifted = jnp.concatenate(
            [jnp.zeros((offset,) + signal.shape[1:], signal.dtype), signal[: length - offset]],
            axis=0,
        )
        earlier = jnp.concatenate(
            [jnp.full((offset,), -1, jnp.int32), segment[: length - offset]], axis=0
        )
        same_doc = jnp.where(earlier == segment, 1.0, 0.0).astype(signal.dtype)
        result = result + weight[tap_count - 1 - offset] * shifted * same_doc[:, None, None]
    return result


def unit_lower_inverse(lower_part):
    size = lower_part.shape[-1]
    identity = jnp.eye(size, dtype=lower_part.dtype)[None]
    inverse = identity - lower_part
    power = lower_part
    reach = 2
    while reach < size:
        power = jnp.einsum("hij,hjk->hik", power, power, precision=highest)
        inverse = jnp.einsum("hij,hjk->hik", inverse, identity + power, precision=highest)
        reach = reach * 2
    return inverse


def span_step(state_pair, blocks):
    memory, last_seen = state_pair
    queries, key_rows, value_rows, decays, beta_rows, segment = blocks
    block_len = segment.shape[0]
    cumulative = jnp.cumsum(decays, axis=0)
    same_doc = segment[:, None] == segment[None, :]
    row_index = lax.broadcasted_iota(jnp.int32, (block_len, block_len), 0)
    col_index = lax.broadcasted_iota(jnp.int32, (block_len, block_len), 1)
    strict_mask = (same_doc & (row_index > col_index))[:, :, None]
    within_mask = (same_doc & (row_index >= col_index))[:, :, None]
    log_gap = cumulative[:, None, :] - cumulative[None, :, :]
    strict_decay = jnp.where(strict_mask, jnp.exp(jnp.where(strict_mask, log_gap, 0.0)), 0.0)
    within_decay = jnp.where(within_mask, jnp.exp(jnp.where(within_mask, log_gap, 0.0)), 0.0)
    carry_on = segment == last_seen
    start_scale = jnp.where(carry_on[:, None], jnp.exp(cumulative), 0.0)
    key_dots = jnp.einsum("ihd,jhd->hij", key_rows, key_rows, precision=highest)
    lower_part = key_dots * (strict_decay * beta_rows[:, None, :]).transpose(2, 0, 1)
    inverse = unit_lower_inverse(lower_part)
    carried = jnp.einsum("ihk,hvk->ihv", key_rows, memory, precision=highest)
    target = beta_rows[:, :, None] * (value_rows - start_scale[:, :, None] * carried)
    pseudo = jnp.einsum("hij,jhv->hiv", inverse, target, precision=highest)
    scores = jnp.einsum(
        "ihd,jhd->hij", queries, key_rows, precision=highest
    ) * within_decay.transpose(2, 0, 1)
    output = jnp.einsum("hij,hjv->ihv", scores, pseudo, precision=highest)
    output = output + start_scale[:, :, None] * jnp.einsum(
        "ihk,hvk->ihv", queries, memory, precision=highest
    )
    last_doc = segment[block_len - 1]
    end_scale = jnp.where(
        (segment == last_doc)[:, None],
        jnp.exp(cumulative[block_len - 1][None, :] - cumulative),
        0.0,
    )
    whole_keep = jnp.where(carry_on[block_len - 1], jnp.exp(cumulative[block_len - 1]), 0.0)
    memory = whole_keep[:, None, None] * memory + jnp.einsum(
        "hiv,ih,ihk->hvk", pseudo, end_scale, key_rows, precision=highest
    )
    return ((memory, last_doc), output)


def delta_rule(queries, key_rows, value_rows, decays, beta_rows, segment):
    full_length, head_count, value_width = value_rows.shape
    block_count = full_length // SPAN

    def to_blocks(stacked):
        return stacked.reshape((block_count, SPAN) + stacked.shape[1:])

    memory = jnp.zeros((head_count, value_width, key_rows.shape[2]), value_rows.dtype)
    no_doc = jnp.full((), -1, jnp.int32)
    last_pair, outputs = lax.scan(
        jax.checkpoint(span_step),
        (memory, no_doc),
        (
            to_blocks(queries),
            to_blocks(key_rows),
            to_blocks(value_rows),
            to_blocks(decays),
            to_blocks(beta_rows),
            to_blocks(segment),
        ),
    )
    return outputs.reshape(full_length, head_count, value_width)


def mixer(projected, rate_logits, conv_weight, a_log, out_gain, segment):
    queries = jax.nn.silu(short_conv(projected[:, 0], conv_weight[0], segment))
    key_rows = jax.nn.silu(short_conv(projected[:, 1], conv_weight[1], segment))
    value_rows = jax.nn.silu(short_conv(projected[:, 2], conv_weight[2], segment))
    queries = (
        queries
        * lax.rsqrt(jnp.sum(queries * queries, axis=-1, keepdims=True) + unit_eps)
        * queries.shape[-1] ** (-0.5)
    )
    key_rows = key_rows * lax.rsqrt(jnp.sum(key_rows * key_rows, axis=-1, keepdims=True) + unit_eps)
    beta_rows = jax.nn.sigmoid(rate_logits[:, 1])
    decays = -jnp.exp(a_log) * jax.nn.softplus(rate_logits[:, 0])
    mixed_out = delta_rule(queries, key_rows, value_rows, decays, beta_rows, segment)
    mixed_out = (
        mixed_out
        * lax.rsqrt(jnp.mean(mixed_out * mixed_out, axis=-1, keepdims=True) + norm_eps)
        * out_gain
        * jax.nn.silu(projected[:, 3])
    )
    return mixed_out.reshape(mixed_out.shape[0], -1)


def local(
    tokens,
    segment_ids,
    norm_gains,
    w_mixer_in,
    w_rates,
    conv_weight,
    a_log,
    out_gain,
    w_output,
    w_gate_up,
    w_down,
    cotangent,
):
    tensor_rank = lax.axis_index("tensor")
    gathered = (
        lax.all_gather(w_mixer_in, "dp", axis=0, tiled=True),
        lax.all_gather(w_rates, "dp", axis=0, tiled=True),
        lax.all_gather(conv_weight, "dp", axis=3, tiled=True),
        lax.all_gather(w_output, "dp", axis=1, tiled=True),
        lax.all_gather(w_gate_up, "dp", axis=0, tiled=True),
        lax.all_gather(w_down, "dp", axis=1, tiled=True),
    )
    mix_full, rate_full, conv_full, out_full, up_full, down_full = gathered
    model_width = mix_full.shape[0]
    head_here = rate_full.shape[2]
    hidden_here = up_full.shape[2]
    segment = segment_ids[0]
    local_log = lax.dynamic_slice_in_dim(a_log, tensor_rank * head_here, head_here)
    inputs = tokens[0].astype(jnp.float32)
    normed, first_back = jax.vjp(first_norm, inputs, norm_gains)
    normed_all = lax.all_gather(normed.astype(jnp.bfloat16), "tensor", axis=0, tiled=True)
    full_length = normed_all.shape[0]
    projected = jnp.dot(
        normed_all, mix_full.reshape(model_width, -1), preferred_element_type=jnp.float32
    )
    rate_logits = jnp.dot(
        normed_all, rate_full.reshape(model_width, -1), preferred_element_type=jnp.float32
    )

    def local_mixer(projection, rate_input, conv_input, log_input, gain_input):
        return mixer(projection, rate_input, conv_input, log_input, gain_input, segment)

    mixed_out, mixer_back = jax.vjp(
        local_mixer,
        projected.reshape(full_length, 4, head_here, -1),
        rate_logits.reshape(full_length, 2, head_here),
        conv_full.astype(jnp.float32),
        local_log,
        out_gain,
    )
    mixed_low = mixed_out.astype(jnp.bfloat16)
    picked = mixed_low
    residual = inputs + lax.psum_scatter(
        jnp.dot(picked, out_full, preferred_element_type=jnp.float32).astype(jnp.bfloat16),
        "tensor",
        scatter_dimension=0,
        tiled=True,
    ).astype(jnp.float32)
    normed_ffn, second_back = jax.vjp(second_norm, residual, norm_gains)
    ffn_all = lax.all_gather(normed_ffn.astype(jnp.bfloat16), "tensor", axis=0, tiled=True)
    gate_up = jnp.dot(
        ffn_all, up_full.reshape(model_width, -1), preferred_element_type=jnp.float32
    ).reshape(full_length, 2, hidden_here)
    hidden_raw, swish_back = jax.vjp(swish_product, gate_up)
    hidden = hidden_raw.astype(jnp.bfloat16)
    picked = hidden
    result = residual + lax.psum_scatter(
        jnp.dot(picked, down_full, preferred_element_type=jnp.float32).astype(jnp.bfloat16),
        "tensor",
        scatter_dimension=0,
        tiled=True,
    ).astype(jnp.float32)
    out_tokens = result.astype(jnp.bfloat16)[None]
    regathered = (
        lax.all_gather(w_mixer_in, "dp", axis=0, tiled=True),
        lax.all_gather(w_rates, "dp", axis=0, tiled=True),
        lax.all_gather(w_output, "dp", axis=1, tiled=True),
        lax.all_gather(w_gate_up, "dp", axis=0, tiled=True),
        lax.all_gather(w_down, "dp", axis=1, tiled=True),
    )
    mix_weight, rate_weight, out_weight, up_weight, down_weight = regathered
    grad_local = cotangent[0]
    grad_all = lax.all_gather(grad_local, "tensor", axis=0, tiled=True)
    hidden_grad = contract_last(grad_all, down_weight)
    down_grad = contract_first(hidden, grad_all)
    (gate_up_grad,) = swish_back(hidden_grad)
    gate_up_low = gate_up_grad.reshape(full_length, -1).astype(jnp.bfloat16)
    up_flat = up_weight.reshape(model_width, -1)
    up_grad = contract_first(ffn_all, gate_up_low).reshape(model_width, 2, hidden_here)
    picked = gate_up_low
    ffn_input_grad = lax.psum_scatter(
        contract_last(picked, up_flat).astype(jnp.bfloat16),
        "tensor",
        scatter_dimension=0,
        tiled=True,
    ).astype(jnp.float32)
    residual_part, second_gains = second_back(ffn_input_grad)
    residual_grad = grad_local.astype(jnp.float32) + residual_part
    residual_all = lax.all_gather(residual_grad.astype(jnp.bfloat16), "tensor", axis=0, tiled=True)
    mixed_grad = contract_last(residual_all, out_weight)
    out_grad = contract_first(mixed_low, residual_all)
    projection_grad, rate_grad, conv_grad, log_grad, gain_grad = mixer_back(mixed_grad)
    projection_low = projection_grad.reshape(full_length, -1).astype(jnp.bfloat16)
    rate_low = rate_grad.reshape(full_length, -1).astype(jnp.bfloat16)
    mix_flat = mix_weight.reshape(model_width, -1)
    rate_flat = rate_weight.reshape(model_width, -1)
    mix_grad = contract_first(normed_all, projection_low).reshape(mix_weight.shape)
    rate_weight_grad = contract_first(normed_all, rate_low).reshape(rate_weight.shape)
    picked = projection_low
    mixer_input_grad = lax.psum_scatter(
        (contract_last(picked, mix_flat) + contract_last(rate_low, rate_flat)).astype(jnp.bfloat16),
        "tensor",
        scatter_dimension=0,
        tiled=True,
    ).astype(jnp.float32)
    input_part, first_gains = first_back(mixer_input_grad)
    input_grad = (residual_grad + input_part).astype(jnp.bfloat16)[None]
    log_full = lax.dynamic_update_slice_in_dim(
        jnp.zeros(a_log.shape, jnp.float32), log_grad, tensor_rank * head_here, 0
    )
    small_sums = lax.psum((first_gains + second_gains, gain_grad, log_full), ("dp", "tensor"))
    owned_grads = (
        lax.psum_scatter(
            mix_grad.astype(jnp.bfloat16), "dp", scatter_dimension=0, tiled=True
        ).astype(jnp.float32),
        lax.psum_scatter(
            rate_weight_grad.astype(jnp.bfloat16), "dp", scatter_dimension=0, tiled=True
        ).astype(jnp.float32),
        lax.psum_scatter(
            conv_grad.astype(jnp.bfloat16), "dp", scatter_dimension=3, tiled=True
        ).astype(jnp.float32),
        lax.psum_scatter(
            out_grad.astype(jnp.bfloat16), "dp", scatter_dimension=1, tiled=True
        ).astype(jnp.float32),
        lax.psum_scatter(
            up_grad.astype(jnp.bfloat16), "dp", scatter_dimension=0, tiled=True
        ).astype(jnp.float32),
        lax.psum_scatter(
            down_grad.astype(jnp.bfloat16), "dp", scatter_dimension=1, tiled=True
        ).astype(jnp.float32),
    )
    return (
        out_tokens,
        input_grad,
        small_sums[0],
        owned_grads[0],
        owned_grads[1],
        owned_grads[2],
        small_sums[2],
        small_sums[1],
        owned_grads[3],
        owned_grads[4],
        owned_grads[5],
    )


def solution(mesh):
    in_specs = (
        P("dp", "tensor", None),
        P("dp", None),
        P(),
        P("dp", None, "tensor", None),
        P("dp", None, "tensor"),
        P(None, None, "tensor", "dp"),
        P(),
        P(),
        P("tensor", "dp"),
        P("dp", None, "tensor"),
        P("tensor", "dp"),
        P("dp", "tensor", None),
    )
    out_specs = (
        P("dp", "tensor", None),
        P("dp", "tensor", None),
        P(),
        P("dp", None, "tensor", None),
        P("dp", None, "tensor"),
        P(None, None, "tensor", "dp"),
        P(),
        P(),
        P("tensor", "dp"),
        P("dp", None, "tensor"),
        P("tensor", "dp"),
    )
    return jax.shard_map(local, mesh=mesh, in_specs=in_specs, out_specs=out_specs, check_vma=False)
```

profile of v0, /device:TPU:0, one launch (start us, length us, event | category | flops | bytes accessed | tf_op | source)
XLA Modules:
  0.0 1681.1 jit_solution(323068298652197)
XLA Ops:
  14.1 24.1 %all_gather.37 = bf16[3,4,4,128]{2,1,0,3:T(4,128)(2,1)S(1)} all-gather(bf16[3,4,4,8]{2,1,0,3:T(4,128)(2,1)S(1)} %copy.493), channel_id=1, replica_groups=mesh['dp'=16,'tensor'=2] {'dp'}, dimensions={3}, use_global_device_ids=true | all-gather | bytes 13056 | tf_op jit(solution)/shard_map/all_gather | solution.py:177
  40.0 19.1 %all_gather.36 = bf16[1024,2,4]{2,1,0:T(2,128)(2,1)S(1)} all-gather(bf16[64,2,4]{2,1,0:T(2,128)(2,1)S(1)} %copy.486), channel_id=1, replica_groups=mesh['dp'=16,'tensor'=2] {'dp'}, dimensions={0}, use_global_device_ids=true | all-gather | bytes 17408 | tf_op jit(solution)/shard_map/all_gather | solution.py:176
  65.2 36.3 %all-gather.12.cloned.1.call-done = bf16[1024,4,4,128]{3,0,2,1:T(8,128)(2,1)} async-done(((bf16[64,4,4,128]{3,0,2,1:T(8,128)(2,1)}), bf16[1024,4,4,128]{3,0,2,1:T(8,128)(2,1)}) %all-gather.12.cloned.1.call-update) | async-done | bytes 4194320 | tf_op jit(solution)/shard_map/all_gather | solution.py:175
  137.2 253.9 %while.48 = (s32[]{:T(128)}, f32[4,128,128]{2,1,0:T(8,128)S(1)}, s32[]{:T(128)}, f32[16,64,4,128]{3,1,2,0:T(8,128)S(1)}, f32[16,4,128,128]{3,2,1,0:T(8,128)}, /*...) while((s32[]{:T(128)}, f32[4,128,128]{2,1,0:T(8,128)S(1)}, ...), condition=%wide.region_5.6_spmd.clone.clone, body=%wide.region_3.5_spmd.clone.clone.sunk | while | flops 378368640 | bytes 5600305 | solution.py:122
  416.4 28.7 %reduce-scatter.13.cloned.1.call-done = bf16[512,1024]{1,0:T(8,128)(2,1)} async-done(((bf16[1024,1024]{1,0:T(8,128)(2,1)}), bf16[512,1024]{1,0:T(8,128)(2,1)}) %reduce-scatter.13.cloned.1.call-update) | async-done | bytes 1048592 | tf_op jit(solution)/shard_map/reduce_scatter | solution.py:212
  449.8 57.4 %all-gather.18.cloned.1.call-done = bf16[1024,2,1408]{2,0,1:T(8,128)(2,1)} async-done(((bf16[64,2,1408]{2,0,1:T(8,128)(2,1)}), bf16[1024,2,1408]{2,0,1:T(8,128)(2,1)}) %all-gather.18.cloned.1.call-update) | async-done | bytes 5767184 | tf_op jit(solution)/shard_map/all_gather | solution.py:179
  507.1 8.6 copy.519
  515.7 25.2 %all-gather.16.cloned.1.call-done = bf16[1024,1024]{1,0:T(8,128)(2,1)} async-done(((bf16[512,1024]{1,0:T(8,128)(2,1)}), bf16[1024,1024]{1,0:T(8,128)(2,1)}) %all-gather.16.cloned.1.call-update) | async-done | bytes 2097168 | tf_op jit(solution)/shard_map/all_gather | solution.py:219
  540.9 11.9 fusion.190
  552.8 22.9 %all-gather.24.cloned.1.call-done = bf16[1,1024,1024]{2,1,0:T(8,128)(2,1)} async-done(((bf16[1,512,1024]{2,1,0:T(8,128)(2,1)}), bf16[1,1024,1024]{2,1,0:T(8,128)(2,1)}) %all-gather.24.cloned.1.call-update) | async-done | bytes 2097168 | tf_op jit(solution)/shard_map/all_gather | solution.py:242
  575.7 46.9 %all-gather.20.cloned.1.call-done = bf16[1408,1024]{0,1:T(8,128)(2,1)} async-done(((bf16[1408,64]{0,1:T(8,128)(2,1)}), bf16[1408,1024]{0,1:T(8,128)(2,1)}) %all-gather.20.cloned.1.call-update) | async-done | bytes 2883600 | tf_op jit(solution)/shard_map/all_gather | solution.py:180
  622.6 12.9 multiply_bitcast_fusion
  642.9 9.2 bitcast_convert_fusion
  652.2 30.2 %reduce-scatter.17.cloned.1.call-done = bf16[512,1024]{1,0:T(8,128)(2,1)} async-done(((bf16[1024,1024]{1,0:T(8,128)(2,1)}), bf16[512,1024]{1,0:T(8,128)(2,1)}) %reduce-scatter.17.cloned.1.call-update) | async-done | bytes 1048592 | tf_op jit(solution)/shard_map/reduce_scatter | solution.py:250
  695.5 25.4 %all-gather.22.cloned.1.call-done = bf16[1024,1024]{1,0:T(8,128)(2,1)} async-done(((bf16[512,1024]{1,0:T(8,128)(2,1)}), bf16[1024,1024]{1,0:T(8,128)(2,1)}) %all-gather.22.cloned.1.call-update) | async-done | bytes 2097168 | tf_op jit(solution)/shard_map/all_gather | solution.py:258
  750.1 570.7 %while.47 = (s32[]{:T(128)}, f32[4,128,128]{2,1,0:T(8,128)S(1)}, f32[16,64,4,128]{3,1,0,2:T(8,128)}, f32[16,64,4,128]{3,1,0,2:T(8,128)}, f32[16,64,4,128]{3,1,0,...) while((s32[]{:T(128)}, f32[4,128,128]{2,1,0:T(8,128)S(1)}, ...), condition=%wide.region_24.25_spmd.clone, body=%wide.region_13.24_spmd.clone.sunk | while | flops 1059863936 | bytes 19563816 | solution.py:122
  1340.9 10.8 fusion.193
  1360.5 13.3 multiply_reduce_fusion.15
  1401.8 9.0 multiply_reduce_fusion.12
  1447.0 62.5 %all-reduce.47 = bf16[3,4,4,128]{3,2,1,0:T(4,128)(2,1)S(1)} all-reduce(bf16[3,4,4,128]{3,2,1,0:T(4,128)(2,1)S(1)} %add_convert_fusion.4), channel_id=9, replica_groups=mesh['dp'=16,'tensor'=2] {'dp'}, use_global_device_ids=true, to_apply=%region_46.47.clone | all-reduce | flops 6144 | bytes 24576
  1515.0 13.2 reduce-scatter.25.cloned.1.call-done
  1530.5 30.9 %reduce-scatter.19.cloned.1.call-done = bf16[512,1024]{1,0:T(8,128)(2,1)} async-done(((bf16[1024,1024]{1,0:T(8,128)(2,1)}), bf16[512,1024]{1,0:T(8,128)(2,1)}) %reduce-scatter.19.cloned.1.call-update) | async-done | bytes 1048592 | tf_op jit(solution)/shard_map/reduce_scatter | solution.py:269
  1563.5 39.8 %all-reduce.48 = (f32[2,1024]{1,0:T(2,128)}, f32[8]{0:T(128)}, f32[128]{0:T(128)}) all-reduce(f32[2,1024]{1,0:T(2,128)S(1)} %pad_add_fusion, f32[8]{0:T(128)S(1)} %multiply_dynamic-update-slice_fusion, f32[128]{0:T(128)S(1)} %copy-done.116), channel_id=1, replica_groups=mesh['dp'=16,'tensor'=2] {'dp','tensor'}, use_global_device_ids=true, to_apply=%region_31.32 | all-reduce | flops 2184 | bytes 17472 | tf_op jit(solution)/shard_map/psum | solution.py:280
  1607.5 64.8 %reduce-scatter.21.cloned.1.call-done = bf16[64,4,4,128]{3,0,2,1:T(8,128)(2,1)} async-done(((bf16[1024,4,4,128]{3,0,2,1:T(8,128)(2,1)}), bf16[64,4,4,128]{3,0,2,1:T(8,128)(2,1)}) %reduce-scatter.21.cloned.1.call-update) | async-done | bytes 262160 | tf_op jit(solution)/shard_map/reduce_scatter | solution.py:282
  (2404 shorter events, 1040.4 us)
Async XLA Ops:
  7.2 53.7 %all-gather.10.cloned.1.call-start = ((), (), s32[]{:S(2)}) async-start(), calls=%async_computation.9 | async-start | bytes 3145728 | tf_op jit(solution)/shard_map/all_gather | solution.py:190
  8.0 677.7 %copy-start.67 = (f32[1,1024]{1,0:T(1,128)}, f32[1,1024]{1,0:T(1,128)S(1)}, u32[]{:S(2)}) copy-start(f32[1,1024]{1,0:T(1,128)S(1)} %get-tuple-element.1104) | copy-start | bytes 12292
  12.2 89.3 %all-gather.12.cloned.1.call-start = ((), (), s32[]{:S(2)}) async-start(), calls=%async_computation.10 | async-start | bytes 4456448 | tf_op jit(solution)/shard_map/all_gather | solution.py:175
  13.1 396.7 %all-gather.14.cloned.1.call-start = ((), (), s32[]{:S(2)}) async-start(), calls=%async_computation.11 | async-start | bytes 1114112 | tf_op jit(solution)/shard_map/all_gather | solution.py:178
  13.8 431.2 %reduce-scatter.13.cloned.1.call-start = ((), (), s32[]{:S(2)}) async-start(), calls=%async_computation.12 | async-start | bytes 3145728 | tf_op jit(solution)/shard_map/reduce_scatter | solution.py:212
  391.1 347.7 %copy-start.3 = (f32[16,64,4,128]{3,1,2,0:T(8,128)}, f32[16,64,4,128]{3,1,2,0:T(8,128)S(1)}, u32[]{:S(2)}) copy-start(f32[16,64,4,128]{3,1,2,0:T(8,128)S(1)} %get-tuple-element.542) | copy-start | bytes 6291460
  414.6 92.6 %all-gather.18.cloned.1.call-start = ((), (), s32[]{:S(2)}) async-start(), calls=%async_computation.14 | async-start | bytes 6127616 | tf_op jit(solution)/shard_map/all_gather | solution.py:179
  416.3 124.6 %all-gather.16.cloned.1.call-start = ((), (), s32[]{:S(2)}) async-start(), calls=%async_computation.13 | async-start | bytes 3145728 | tf_op jit(solution)/shard_map/all_gather | solution.py:219
  446.8 238.9 %copy-start.79 = (f32[512]{0:T(512)}, f32[512]{0:T(512)S(1)}, u32[]{:S(2)}) copy-start(f32[512]{0:T(512)S(1)} %fusion.267) | copy-start | bytes 6148
  448.2 127.5 %all-gather.24.cloned.1.call-start = ((), (), s32[]{:S(2)}) async-start(), calls=%async_computation.24 | async-start | bytes 3145728 | tf_op jit(solution)/shard_map/all_gather | solution.py:242
  449.0 173.7 %all-gather.20.cloned.1.call-start = ((), (), s32[]{:S(2)}) async-start(), calls=%async_computation.15 | async-start | bytes 3063808 | tf_op jit(solution)/shard_map/all_gather | solution.py:180
  449.7 232.7 %reduce-scatter.17.cloned.1.call-start = ((), (), s32[]{:S(2)}) async-start(), calls=%async_computation.17 | async-start | bytes 3145728 | tf_op jit(solution)/shard_map/reduce_scatter | solution.py:250
  652.2 68.7 %all-gather.22.cloned.1.call-start = ((), (), s32[]{:S(2)}) async-start(), calls=%async_computation.18 | async-start | bytes 3145728 | tf_op jit(solution)/shard_map/all_gather | solution.py:258
  687.6 757.7 %reduce-scatter.27.cloned.1.call-start = ((), (), s32[]{:S(2)}) async-start(), calls=%async_computation.23 | async-start | bytes 3063808 | tf_op jit(solution)/shard_map/reduce_scatter | solution.py:297
  695.5 816.7 %reduce-scatter.29.cloned.1.call-start = ((), (), s32[]{:S(2)}) async-start(), calls=%async_computation.25 | async-start | bytes 278528
  750.1 572.9 %copy-start.64 = (f32[1024,1,4]{0,2,1:T(4,128)S(1)}, f32[1024,1,4]{0,2,1:T(4,128)}, u32[]{:S(2)}) copy-start(f32[1024,1,4]{0,2,1:T(4,128)} %copy-done.63) | copy-start | bytes 49156
  1326.8 186.8 %reduce-scatter.23.cloned.1.call-start = ((), (), s32[]{:S(2)}) async-start(), calls=%async_computation.21 | async-start | bytes 1114112 | tf_op jit(solution)/shard_map/reduce_scatter | solution.py:291
  1330.9 197.4 %reduce-scatter.25.cloned.1.call-start = ((), (), s32[]{:S(2)}) async-start(), calls=%async_computation.22 | async-start | bytes 6127616 | tf_op jit(solution)/shard_map/reduce_scatter | solution.py:294
  1351.7 209.6 %reduce-scatter.19.cloned.1.call-start = ((), (), s32[]{:S(2)}) async-start(), calls=%async_computation.19 | async-start | bytes 3145728 | tf_op jit(solution)/shard_map/reduce_scatter | solution.py:269
  1422.3 181.0 %reduce-scatter.15.cloned.1.call-start = ((), (), s32[]{:S(2)}) async-start(), calls=%async_computation.16 | async-start | bytes 3145728 | tf_op jit(solution)/shard_map/reduce_scatter | solution.py:226
  1428.9 243.4 %reduce-scatter.21.cloned.1.call-start = ((), (), s32[]{:S(2)}) async-start(), calls=%async_computation.20 | async-start | bytes 4456448 | tf_op jit(solution)/shard_map/reduce_scatter | solution.py:282
  1443.4 117.9 %copy-start.2 = (bf16[1,512,1024]{2,1,0:T(8,128)(2,1)S(1)}, bf16[1,512,1024]{2,1,0:T(8,128)(2,1)}, u32[]{:S(2)}) copy-start(bf16[1,512,1024]{2,1,0:T(8,128)(2,1)} %param.16) | copy-start | bytes 3145732
  1443.4 117.9 %copy-start.74 = (f32[1,1024]{1,0:T(1,128)S(1)}, f32[1,1024]{1,0:T(1,128)}, u32[]{:S(2)}) copy-start(f32[1,1024]{1,0:T(1,128)} %copy-done.73) | copy-start | bytes 12292
  1443.4 117.9 %copy-start.82 = (f32[512]{0:T(512)S(1)}, f32[512]{0:T(512)}, u32[]{:S(2)}) copy-start(f32[512]{0:T(512)} %copy-done.81) | copy-start | bytes 6148
  (136 other events, 2797.3 us)
Sparse Core Ops, SparseCore 0:
  12.3 35.8 all-gather.9
  50.9 50.5 all-gather.11
  103.7 36.4 all-gather.13
  414.7 30.3 reduce-scatter.12
  448.0 59.0 all-gather.17
  509.2 31.7 all-gather.15
  542.5 33.1 all-gather.23
  578.2 44.3 all-gather.19
  652.3 30.1 reduce-scatter.16
  687.7 33.1 all-gather.21
  724.7 65.2 reduce-scatter.26
  1326.9 55.2 reduce-scatter.28
  1386.8 56.4 reduce-scatter.22
  1447.0 81.2 reduce-scatter.24
  1530.4 30.9 reduce-scatter.18
  1563.5 32.4 reduce-scatter.14
  1599.7 72.6 reduce-scatter.20
where the time goes:
time: 1690 us; the launch traced here: 1680 us
  matrix products  598 us (35%)
  waiting for transfers between devices  384 us (23%)
  local copies, waits for them, and re-layouts  299 us (18%)
  other arithmetic  216 us (13%)
  blocking collectives  145 us (9%)
  loops' own time  21.3 us (1%)
    dot_general x320, matrix products, unit_lower_inverse(): power = jnp.einsum('hij,hjk->hik', power, power, precision=highest)  106 us
    dot_general x320, matrix products, unit_lower_inverse(): jnp.einsum('hij,hjk->hik', inverse, identity + power, precision=highest)  105 us
    squeeze x112, local copies, waits for them, and re-layouts, delta_rule(): lax.scan(jax.checkpoint(span_step), (memory, no_doc), (to_blocks(queries)...  81.6 us
    reduce_scatter x1, waiting for transfers between devices, local(): lax.psum_scatter(mix_grad.astype(jnp.bfloat16), 'dp', scatter_dimension=0...  64.8 us
    dot_general x64, matrix products, span_step(): carried = jnp.einsum('ihk,hvk->ihv', key_rows, memory, precision=highest)  63.8 us
    dot_general x64, matrix products, span_step(): jnp.einsum('ihk,hvk->ihv', queries, memory, precision=highest)  63 us
    unnamed x1, blocking collectives  62.5 us
    all_gather x1, waiting for transfers between devices, local(): lax.all_gather(w_gate_up, 'dp', axis=0, tiled=True)  57.4 us
  transfers between devices with their start and end apart: 17, of which 11 were waited for; matrix products, arithmetic and copies ran while one was open for 62% of the time, Pallas kernels for 0%

commit v1 on v0

v1 whole, which is shorter than its diff:
```python
import functools

import jax
import jax.numpy as jnp
from jax import lax
from jax.experimental import pallas as pl
from jax.experimental.pallas import tpu as pltpu
from jax.sharding import PartitionSpec as P

CHUNK = 128
WIDTH = 128
HALO = 8
norm_eps = 1e-05
unit_eps = 1e-06
f32 = jnp.float32
bf16 = jnp.bfloat16

NN = ((1,), (0,))
NT = ((1,), (1,))
TN = ((0,), (0,))


def dot(left, right, dims):
    return lax.dot_general(
        left.astype(bf16), right.astype(bf16), (dims, ((), ())), preferred_element_type=f32
    )


def dot_exact(left, right, dims):
    return lax.dot_general(
        left, right, (dims, ((), ())), precision=lax.Precision.HIGHEST, preferred_element_type=f32
    )


def sigmoid(value):
    return 1.0 / (1.0 + jnp.exp(-value))


def softplus(value):
    return jnp.maximum(value, 0.0) + jnp.log(1.0 + jnp.exp(-jnp.abs(value)))


def shifted(rows, offset):
    return pltpu.roll(rows, offset, 0)[HALO:] if offset else rows[HALO:]


def conv_terms(rows, keeps):
    return [rows[HALO:]] + [
        jnp.where(keeps[offset], shifted(rows, offset), 0.0) for offset in range(1, 4)
    ]


def conv_sum(terms, conv_ref, part, lanes):
    total = None
    for offset in range(4):
        weight = conv_ref[pl.ds(part * 4 + 3 - offset, 1), lanes]
        term = weight * terms[offset]
        total = term if total is None else total + term
    return total


def lane_column(values, lane):
    return jnp.broadcast_to(values[:, lane : lane + 1], values.shape)


def grids():
    row = lax.broadcasted_iota(jnp.int32, (CHUNK, CHUNK), 0)
    col = lax.broadcasted_iota(jnp.int32, (CHUNK, CHUNK), 1)
    return row, col


def level_masks(row, col):
    masks = []
    shift = 0
    while (1 << shift) < CHUNK:
        near = (row >> (shift + 1)) == (col >> (shift + 1))
        apart = (row >> shift) != (col >> shift)
        masks.append(near & apart)
        shift += 1
    return masks


def unit_lower_inverses(lowers, row, col):
    masks = level_masks(row, col)
    identity = jnp.where(row == col, 1.0, 0.0).astype(f32)
    inverses = [identity - jnp.where(masks[0], lower, 0.0) for lower in lowers]
    for mask in masks[1:]:
        blocks = [jnp.where(mask, lower, 0.0) for lower in lowers]
        firsts = [dot(inverse, block, NN) for inverse, block in zip(inverses, blocks)]
        inverses = [inverse - dot(first, inverse, NN) for first, inverse in zip(firsts, inverses)]
    return inverses


def chunk_scales(heads, rates, neg_rate, seg, last_seen, row, col):
    steps = neg_rate * softplus(rates)
    lower_ones = jnp.where(row >= col, 1.0, 0.0).astype(f32)
    cumulative = dot_exact(lower_ones, steps, NN)
    cumulative_rows = cumulative.T
    betas = sigmoid(rates)
    seg_rows = seg.T
    same = seg == seg_rows
    within = same & (row >= col)
    strict = same & (row > col)
    carry = seg == last_seen
    ends = seg == seg[CHUNK - 1 :, :]
    scales = []
    for head in range(heads):
        cum = lane_column(cumulative, head)
        cum_row = cumulative_rows[head : head + 1, :]
        gap = jnp.exp(jnp.minimum(cum - cum_row, 0.0))
        last = cum[CHUNK - 1 :, :]
        scales.append(
            dict(
                beta=lane_column(betas, heads + head),
                within=jnp.where(within, gap, 0.0),
                strict=jnp.where(strict, gap, 0.0),
                start=jnp.where(carry, jnp.exp(cum), 0.0),
                end=jnp.where(ends, jnp.exp(jnp.minimum(last - cum, 0.0)), 0.0),
                keep=jnp.where(carry[CHUNK - 1 :, :], jnp.exp(last), 0.0),
            )
        )
    return scales, steps, betas


def forward_kernel(
    heads, proj_ref, seg_ref, conv_ref, rate_ref, gain_ref,
    mixed_ref, inverse_ref, w_ref, pseudo_ref, out_ref, state_ref,
    state, halo, seg_halo,
):
    step = pl.program_id(0)

    @pl.when(step == 0)
    def _():
        state[...] = jnp.zeros_like(state)
        halo[...] = jnp.zeros_like(halo)
        seg_halo[...] = jnp.full_like(seg_halo, -1.0)

    row, col = grids()
    seg = seg_ref[...]
    seg_rows = jnp.concatenate([seg_halo[...], seg], axis=0)
    keeps = [None] + [shifted(seg_rows, offset) == seg for offset in range(1, 4)]
    last_seen = seg_halo[HALO - 1 :, :]
    wide = heads * WIDTH
    rates = proj_ref[:, 4 * wide : 4 * wide + WIDTH]
    scales, _, _ = chunk_scales(heads, rates, rate_ref[...], seg, last_seen, row, col)

    queries, keys, values = [], [], []
    for head in range(heads):
        for part, into in ((0, queries), (1, keys), (2, values)):
            at = part * wide + head * WIDTH
            lanes = slice(at, at + WIDTH)
            rows = jnp.concatenate([halo[:, lanes], proj_ref[:, lanes]], axis=0)
            terms = conv_terms(rows, keeps)
            total = conv_sum(terms, conv_ref, part, slice(head * WIDTH, (head + 1) * WIDTH))
            into.append(total * sigmoid(total))
    for head in range(heads):
        query, key = queries[head], keys[head]
        queries[head] = query * (
            lax.rsqrt(jnp.sum(query * query, axis=-1, keepdims=True) + unit_eps) * WIDTH**-0.5
        )
        keys[head] = key * lax.rsqrt(jnp.sum(key * key, axis=-1, keepdims=True) + unit_eps)
    halo[...] = proj_ref[CHUNK - HALO :, : 3 * wide]
    seg_halo[...] = seg[CHUNK - HALO :, :]

    lowers, scores = [], []
    for head in range(heads):
        scale = scales[head]
        both = dot(jnp.concatenate([keys[head], queries[head]], axis=0), keys[head], NT)
        lowers.append(both[:CHUNK] * scale["strict"] * scale["beta"])
        scores.append(both[CHUNK:] * scale["within"])
    inverses = unit_lower_inverses(lowers, row, col)
    for head in range(heads):
        scale = scales[head]
        lanes = slice(head * WIDTH, (head + 1) * WIDTH)
        inverse = inverses[head].astype(bf16)
        inverse_ref[:, lanes] = inverse
        memory = state[head]
        state_ref[0, head] = memory.astype(state_ref.dtype)
        target = jnp.concatenate(
            [scale["beta"] * values[head], scale["beta"] * scale["start"] * keys[head]], axis=1
        )
        solved = dot(inverse, target, NN)
        carried = solved[:, WIDTH:]
        w_ref[:, lanes] = carried.astype(bf16)
        read = dot(
            jnp.concatenate([carried, scale["start"] * queries[head]], axis=0), memory, NN
        )
        pseudo = solved[:, :WIDTH] - read[:CHUNK]
        pseudo_ref[:, lanes] = pseudo.astype(bf16)
        output = dot(scores[head], pseudo, NN) + read[CHUNK:]
        out_ref[:, lanes] = output
        state[head] = scale["keep"] * memory + dot(scale["end"] * keys[head], pseudo, TN)
        gate = proj_ref[:, 3 * wide + head * WIDTH : 3 * wide + (head + 1) * WIDTH]
        unit = output * lax.rsqrt(jnp.mean(output * output, axis=-1, keepdims=True) + norm_eps)
        mixed_ref[:, lanes] = (unit * gain_ref[...] * gate * sigmoid(gate)).astype(bf16)


def backward_kernel(
    heads, proj_ref, seg_ref, seg_before_ref, before_ref, conv_ref, rate_ref, gain_ref, grad_ref,
    inverse_ref, w_ref, pseudo_ref, out_ref, state_ref,
    dproj_ref, dconv_ref, drate_ref, dgain_ref,
    dstate, carry_halo,
):
    step = pl.program_id(0)
    first = step == pl.num_programs(0) - 1

    @pl.when(step == 0)
    def _():
        dstate[...] = jnp.zeros_like(dstate)
        carry_halo[...] = jnp.zeros_like(carry_halo)
        dconv_ref[...] = jnp.zeros_like(dconv_ref)
        drate_ref[...] = jnp.zeros_like(drate_ref)
        dgain_ref[...] = jnp.zeros_like(dgain_ref)

    row, col = grids()
    seg = seg_ref[...]
    seg_before = jnp.where(first, -1.0, seg_before_ref[...])
    seg_rows = jnp.concatenate([seg_before, seg], axis=0)
    keeps = [None] + [shifted(seg_rows, offset) == seg for offset in range(1, 4)]
    last_seen = seg_before[HALO - 1 :, :]
    wide = heads * WIDTH
    rates = proj_ref[:, 4 * wide : 4 * wide + WIDTH]
    neg_rate = rate_ref[...]
    scales, steps, betas = chunk_scales(heads, rates, neg_rate, seg, last_seen, row, col)

    def rows_of(part, head):
        at = part * wide + head * WIDTH
        lanes = slice(at, at + WIDTH)
        return jnp.concatenate([before_ref[:, lanes], proj_ref[:, lanes]], axis=0)

    def signal(part, head):
        terms = conv_terms(rows_of(part, head), keeps)
        total = conv_sum(terms, conv_ref, part, slice(head * WIDTH, (head + 1) * WIDTH))
        gate = sigmoid(total)
        return terms, total, gate

    def signal_back(part, head, terms, total, gate, grad):
        grad = grad * (gate * (1.0 + total * (1.0 - gate)))
        lanes = slice(head * WIDTH, (head + 1) * WIDTH)
        spread = None
        for offset in range(4):
            tap = pl.ds(part * 4 + 3 - offset, 1)
            dconv_ref[tap, lanes] += jnp.sum(grad * terms[offset], axis=0, keepdims=True)
            back = conv_ref[tap, lanes] * grad
            if offset:
                back = jnp.where(keeps[offset], back, 0.0)
            back = jnp.concatenate([jnp.zeros((HALO, WIDTH), f32), back], axis=0)
            if offset:
                back = pltpu.roll(back, CHUNK + HALO - offset, 0)
            spread = back if spread is None else spread + back
        at = part * wide + head * WIDTH
        lanes = slice(at, at + WIDTH)
        tail = jnp.concatenate(
            [jnp.zeros((CHUNK - HALO, WIDTH), f32), carry_halo[:, lanes]], axis=0
        )
        dproj_ref[:, lanes] = (spread[HALO:] + tail).astype(bf16)
        carry_halo[:, lanes] = spread[:HALO]

    lane = col
    cum_columns = jnp.zeros((CHUNK, WIDTH), f32)
    cum_rows = jnp.zeros((CHUNK, CHUNK), f32)
    dbeta_columns = jnp.zeros((CHUNK, WIDTH), f32)
    dgain = jnp.zeros((1, WIDTH), f32)
    for head in range(heads):
        scale = scales[head]
        lanes = slice(head * WIDTH, (head + 1) * WIDTH)
        beta, start, end, keep = scale["beta"], scale["start"], scale["end"], scale["keep"]
        q_terms, q_total, q_gate = signal(0, head)
        k_terms, k_total, k_gate = signal(1, head)
        v_terms, v_total, v_gate = signal(2, head)
        q_act, k_act, value = q_total * q_gate, k_total * k_gate, v_total * v_gate
        q_norm = lax.rsqrt(jnp.sum(q_act * q_act, axis=-1, keepdims=True) + unit_eps)
        k_norm = lax.rsqrt(jnp.sum(k_act * k_act, axis=-1, keepdims=True) + unit_eps)
        q_unit, key = q_act * q_norm, k_act * k_norm
        query = q_unit * WIDTH**-0.5

        gain = gain_ref[...]
        gate_at = slice(3 * wide + head * WIDTH, 3 * wide + (head + 1) * WIDTH)
        gate = proj_ref[:, gate_at]
        gate_s = sigmoid(gate)
        gate_act = gate * gate_s
        grad = grad_ref[:, lanes].astype(f32)
        output = out_ref[:, lanes]
        inv_rms = lax.rsqrt(jnp.mean(output * output, axis=-1, keepdims=True) + norm_eps)
        unit = output * inv_rms
        grad_unit = grad * unit
        dgain = dgain + jnp.sum(grad_unit * gate_act, axis=0, keepdims=True)
        dproj_ref[:, gate_at] = (
            grad_unit * gain * (gate_s * (1.0 + gate * (1.0 - gate_s)))
        ).astype(bf16)
        dunit = grad * (gain * gate_act)
        dout = inv_rms * (dunit - unit * jnp.mean(dunit * unit, axis=-1, keepdims=True))

        both = dot(jnp.concatenate([key, query], axis=0), key, NT)
        lower_raw = both[:CHUNK] * scale["strict"]
        lower = lower_raw * beta
        scores = both[CHUNK:] * scale["within"]
        inverse = inverse_ref[:, lanes]
        pseudo = pseudo_ref[:, lanes]
        memory = state_ref[0, head]
        dmemory = dstate[head]

        dpseudo = dot(scores, dout, TN) + dot(end * key, dmemory, NN)
        start_query = start * query
        dstate[head] = keep * dmemory + dot(
            jnp.concatenate([start_query.astype(bf16), -w_ref[:, lanes]], axis=0),
            jnp.concatenate([dout.astype(bf16), dpseudo.astype(bf16)], axis=0),
            TN,
        )
        solved = dot(inverse, dpseudo, TN)
        reads = dot(jnp.concatenate([dout, solved], axis=0), memory, NT)
        dquery_start = start * reads[:CHUNK]
        dkey_start = -start * reads[CHUNK:]
        by_pseudo = dot(jnp.concatenate([dout, solved], axis=0), pseudo, NT)
        dscores = by_pseudo[:CHUNK]
        dlower = -by_pseudo[CHUNK:]
        dkey_end = end * dot(pseudo, dmemory, NT)

        dbeta = jnp.sum(
            solved * value + dkey_start * key + dlower * lower_raw, axis=-1, keepdims=True
        )
        pair = dscores * scores + dlower * lower
        end_terms = dkey_end * key
        dcum = jnp.sum(
            pair + dquery_start * query + (dkey_start * key) * beta - end_terms,
            axis=-1,
            keepdims=True,
        )
        last_total = jnp.sum(
            jnp.sum(end_terms, axis=0, keepdims=True)
            + keep * jnp.sum(memory * dmemory, axis=0, keepdims=True),
            axis=-1,
            keepdims=True,
        )
        dcum = dcum + jnp.where(row[:, :1] == CHUNK - 1, last_total, 0.0)
        cum_columns = cum_columns + jnp.where(lane == head, dcum, 0.0)
        dbeta_columns = dbeta_columns + jnp.where(lane == heads + head, dbeta, 0.0)
        cum_rows = cum_rows + jnp.where(row == head, jnp.sum(pair, axis=0, keepdims=True), 0.0)

        near = (dlower * (scale["strict"] * beta)).astype(bf16)
        far = (dscores * scale["within"]).astype(bf16)
        toward = dot(jnp.concatenate([near, far], axis=0), key, NN)
        dkey = (
            toward[:CHUNK]
            + dot(
                jnp.concatenate([near, far], axis=0),
                jnp.concatenate([key, query], axis=0),
                TN,
            )
            + beta * dkey_start
            + dkey_end
        )
        dquery = (toward[CHUNK:] + dquery_start) * WIDTH**-0.5
        dvalue = beta * solved
        dq_act = q_norm * (dquery - q_unit * jnp.sum(q_unit * dquery, axis=-1, keepdims=True))
        dk_act = k_norm * (dkey - key * jnp.sum(key * dkey, axis=-1, keepdims=True))
        signal_back(0, head, q_terms, q_total, q_gate, dq_act)
        signal_back(1, head, k_terms, k_total, k_gate, dk_act)
        signal_back(2, head, v_terms, v_total, v_gate, dvalue)

    upper_ones = jnp.where(row <= col, 1.0, 0.0).astype(f32)
    dsteps = dot_exact(upper_ones, cum_columns - cum_rows.T, NN)
    drate_ref[...] += jnp.sum(dsteps * steps, axis=0, keepdims=True)
    dgain_ref[...] += dgain
    dlogits = dsteps * neg_rate * betas + dbeta_columns * betas * (1.0 - betas)
    dproj_ref[:, 4 * wide : 4 * wide + WIDTH] = jnp.where(
        lane < 2 * heads, dlogits, 0.0
    ).astype(bf16)


def mixer_forward(proj, seg_wide, conv_rows, neg_rate, gain):
    length, width = proj.shape
    heads = (width - WIDTH) // (4 * WIDTH)
    wide = heads * WIDTH
    count = length // CHUNK
    by_chunk = lambda cols: pl.BlockSpec((CHUNK, cols), lambda i: (i, 0))
    whole = lambda rows, cols: pl.BlockSpec((rows, cols), lambda i: (0, 0))
    return pl.pallas_call(
        functools.partial(forward_kernel, heads),
        grid=(count,),
        in_specs=[
            by_chunk(width), by_chunk(WIDTH), whole(12, wide), whole(1, WIDTH), whole(1, WIDTH),
        ],
        out_specs=[
            by_chunk(wide), by_chunk(wide), by_chunk(wide), by_chunk(wide), by_chunk(wide),
            pl.BlockSpec((1, heads, WIDTH, WIDTH), lambda i: (i, 0, 0, 0)),
        ],
        out_shape=[
            jax.ShapeDtypeStruct((length, wide), bf16),
            jax.ShapeDtypeStruct((length, wide), bf16),
            jax.ShapeDtypeStruct((length, wide), bf16),
            jax.ShapeDtypeStruct((length, wide), bf16),
            jax.ShapeDtypeStruct((length, wide), f32),
            jax.ShapeDtypeStruct((count, heads, WIDTH, WIDTH), f32),
        ],
        scratch_shapes=[
            pltpu.VMEM((heads, WIDTH, WIDTH), f32),
            pltpu.VMEM((HALO, 3 * wide), f32),
            pltpu.VMEM((HALO, WIDTH), f32),
        ],
        compiler_params=pltpu.CompilerParams(vmem_limit_bytes=48 * 1024 * 1024),
        name="mixer_forward",
    )(proj, seg_wide, conv_rows, neg_rate, gain)


def mixer_backward(proj, seg_wide, conv_rows, neg_rate, gain, grad, saved):
    length, width = proj.shape
    heads = (width - WIDTH) // (4 * WIDTH)
    wide = heads * WIDTH
    count = length // CHUNK
    back = lambda i: count - 1 - i
    by_chunk = lambda cols: pl.BlockSpec((CHUNK, cols), lambda i: (back(i), 0))
    before = lambda cols: pl.BlockSpec(
        (HALO, cols), lambda i: (jnp.maximum(back(i) * (CHUNK // HALO) - 1, 0), 0)
    )
    whole = lambda rows, cols: pl.BlockSpec((rows, cols), lambda i: (0, 0))
    return pl.pallas_call(
        functools.partial(backward_kernel, heads),
        grid=(count,),
        in_specs=[
            by_chunk(width), by_chunk(WIDTH), before(WIDTH), before(3 * wide),
            whole(12, wide), whole(1, WIDTH), whole(1, WIDTH),
            by_chunk(wide), by_chunk(wide), by_chunk(wide), by_chunk(wide), by_chunk(wide),
            pl.BlockSpec((1, heads, WIDTH, WIDTH), lambda i: (back(i), 0, 0, 0)),
        ],
        out_specs=[by_chunk(width), whole(12, wide), whole(1, WIDTH), whole(1, WIDTH)],
        out_shape=[
            jax.ShapeDtypeStruct((length, width), bf16),
            jax.ShapeDtypeStruct((12, wide), f32),
            jax.ShapeDtypeStruct((1, WIDTH), f32),
            jax.ShapeDtypeStruct((1, WIDTH), f32),
        ],
        scratch_shapes=[
            pltpu.VMEM((heads, WIDTH, WIDTH), f32),
            pltpu.VMEM((HALO, 3 * wide), f32),
        ],
        compiler_params=pltpu.CompilerParams(vmem_limit_bytes=48 * 1024 * 1024),
        name="mixer_backward",
    )(proj, seg_wide, seg_wide, proj, conv_rows, neg_rate, gain, grad, *saved)


def rms_norm(values, scales):
    return values * lax.rsqrt(jnp.mean(values * values, axis=-1, keepdims=True) + norm_eps) * scales


def first_norm(values, gains):
    return rms_norm(values, gains[0])


def second_norm(values, gains):
    return rms_norm(values, gains[1])


def swish_product(gate_up):
    return jax.nn.silu(gate_up[:, 0]) * gate_up[:, 1]


def contract_last(operand, other):
    return lax.dot_general(
        operand, other, (((1,), (1,)), ((), ())), preferred_element_type=jnp.float32
    )


def contract_first(operand, other):
    return lax.dot_general(
        operand, other, (((0,), (0,)), ((), ())), preferred_element_type=jnp.float32
    )


def swap(rows):
    return lax.ppermute(rows, "tensor", [(0, 1), (1, 0)])


def local(
    tokens,
    segment_ids,
    norm_gains,
    w_mixer_in,
    w_rates,
    conv_weight,
    a_log,
    out_gain,
    w_output,
    w_gate_up,
    w_down,
    cotangent,
):
    dp_size = lax.axis_size("dp")
    tensor_size = lax.axis_size("tensor")
    tensor_rank = lax.axis_index("tensor")
    rows_here, _, heads, _ = w_mixer_in.shape
    model_width = rows_here * dp_size
    wide = heads * WIDTH
    hidden_here = w_gate_up.shape[2]
    taps_here = conv_weight.shape[3]
    conv_at = 4 * wide + 2 * heads
    out_here = w_output.shape[0]
    own_rows = tokens.shape[1]

    def gather_rows(rows):
        if tensor_size == 2:
            return jnp.concatenate([rows, swap(rows)], axis=0)
        return lax.all_gather(rows, "tensor", axis=0, tiled=True)

    def sum_rows(product):
        if tensor_size == 2:
            return product[:own_rows] + swap(product[own_rows:].astype(bf16)).astype(f32)
        return lax.psum_scatter(
            product.astype(bf16), "tensor", scatter_dimension=0, tiled=True
        ).astype(f32)

    def in_order(rows):
        if tensor_size == 2:
            turned = jnp.concatenate([rows[own_rows:], rows[:own_rows]], axis=0)
            return jnp.where(tensor_rank == 0, rows, turned)
        return rows

    conv_block = jnp.pad(
        conv_weight.transpose(3, 0, 1, 2).reshape(taps_here, 12 * heads),
        ((0, rows_here - taps_here), (0, WIDTH - 14 * heads)),
    )
    mixer_pack = jnp.concatenate(
        [w_mixer_in.reshape(rows_here, -1), w_rates.reshape(rows_here, -1), conv_block], axis=1
    )
    mix_full = lax.all_gather(mixer_pack, "dp", axis=0, tiled=True)
    rest_pack = jnp.concatenate(
        [w_gate_up.reshape(rows_here, -1), w_output.T, w_down.T], axis=1
    )
    rest_full = lax.all_gather(rest_pack, "dp", axis=0, tiled=True)
    up_full = rest_full[:, : 2 * hidden_here]
    out_full = rest_full[:, 2 * hidden_here : 2 * hidden_here + out_here]
    down_full = rest_full[:, 2 * hidden_here + out_here :]
    conv_rows = (
        mix_full[:, conv_at : conv_at + 12 * heads]
        .reshape(dp_size, rows_here, 12 * heads)[:, :taps_here]
        .reshape(dp_size * taps_here, 12 * heads)
        .T.reshape(12, wide)
        .astype(f32)
    )
    segment = jnp.broadcast_to(segment_ids[0][:, None].astype(f32), (segment_ids.shape[1], WIDTH))
    neg_rate = jnp.pad(
        -jnp.exp(lax.dynamic_slice_in_dim(a_log, tensor_rank * heads, heads)), (0, WIDTH - heads)
    )[None]
    gain_row = out_gain[None]

    grad_local = cotangent[0]
    grad_all = gather_rows(grad_local)
    inputs = tokens[0].astype(f32)
    normed, first_back = jax.vjp(first_norm, inputs, norm_gains)
    normed_all = in_order(gather_rows(normed.astype(bf16)))
    projected = jnp.dot(normed_all, mix_full, preferred_element_type=f32)
    mixed, *saved = mixer_forward(projected, segment, conv_rows, neg_rate, gain_row)
    residual = inputs + sum_rows(contract_last(in_order(mixed), out_full))
    normed_ffn, second_back = jax.vjp(second_norm, residual, norm_gains)
    ffn_all = gather_rows(normed_ffn.astype(bf16))
    gate_up = jnp.dot(ffn_all, up_full, preferred_element_type=f32).reshape(-1, 2, hidden_here)
    hidden_raw, swish_back = jax.vjp(swish_product, gate_up)
    hidden = hidden_raw.astype(bf16)
    result = residual + sum_rows(contract_last(hidden, down_full))
    out_tokens = result.astype(bf16)[None]

    hidden_grad = jnp.dot(grad_all, down_full, preferred_element_type=f32)
    down_grad = contract_first(grad_all, hidden)
    (gate_up_grad,) = swish_back(hidden_grad)
    gate_up_low = gate_up_grad.reshape(-1, 2 * hidden_here).astype(bf16)
    up_grad = contract_first(ffn_all, gate_up_low)
    rest_grads = lax.psum_scatter(
        jnp.concatenate([up_grad.astype(bf16), down_grad.astype(bf16)], axis=1),
        "dp",
        scatter_dimension=0,
        tiled=True,
    )
    ffn_input_grad = sum_rows(contract_last(gate_up_low, up_full))
    residual_part, second_gains = second_back(ffn_input_grad)
    residual_grad = grad_local.astype(f32) + residual_part
    residual_all = in_order(gather_rows(residual_grad.astype(bf16)))
    mixed_grad = jnp.dot(residual_all, out_full, preferred_element_type=f32)
    out_grad = contract_first(residual_all, mixed)
    projection_grad, conv_grad, log_grad, gain_grad = mixer_backward(
        projected, segment, conv_rows, neg_rate, gain_row, mixed_grad, saved
    )
    mix_grad = contract_first(normed_all, projection_grad)
    conv_grad = jnp.pad(
        conv_grad.reshape(12 * heads, WIDTH).T.reshape(dp_size, taps_here, 12 * heads),
        ((0, 0), (0, rows_here - taps_here), (0, 0)),
    ).reshape(model_width, 12 * heads)
    mix_grads = lax.psum_scatter(
        jnp.concatenate(
            [
                mix_grad[:, :conv_at].astype(bf16),
                conv_grad.astype(bf16),
                jnp.zeros((model_width, WIDTH - 14 * heads), bf16),
                out_grad.astype(bf16),
            ],
            axis=1,
        ),
        "dp",
        scatter_dimension=0,
        tiled=True,
    ).astype(f32)
    mixer_input_grad = sum_rows(in_order(contract_last(projection_grad, mix_full)))
    input_part, first_gains = first_back(mixer_input_grad)
    input_grad = (residual_grad + input_part).astype(bf16)[None]
    log_full = lax.dynamic_update_slice_in_dim(
        jnp.zeros(a_log.shape, f32), log_grad[0, :heads], tensor_rank * heads, 0
    )
    small = jnp.concatenate(
        [(first_gains + second_gains).reshape(-1), gain_grad.reshape(-1), log_full]
    )
    small = lax.psum(small, ("dp", "tensor"))
    gain_count = 2 * model_width
    rest_grads = rest_grads.astype(f32)
    return (
        out_tokens,
        input_grad,
        small[:gain_count].reshape(2, model_width),
        mix_grads[:, : 4 * wide].reshape(w_mixer_in.shape),
        mix_grads[:, 4 * wide : conv_at].reshape(w_rates.shape),
        mix_grads[:taps_here, conv_at : conv_at + 12 * heads]
        .reshape(taps_here, 3, 4, heads)
        .transpose(1, 2, 3, 0),
        small[gain_count + WIDTH :],
        small[gain_count : gain_count + WIDTH],
        mix_grads[:, 4 * wide + WIDTH :].T,
        rest_grads[:, : 2 * hidden_here].reshape(w_gate_up.shape),
        rest_grads[:, 2 * hidden_here :].T,
    )


def solution(mesh):
    in_specs = (
        P("dp", "tensor", None),
        P("dp", None),
        P(),
        P("dp", None, "tensor", None),
        P("dp", None, "tensor"),
        P(None, None, "tensor", "dp"),
        P(),
        P(),
        P("tensor", "dp"),
        P("dp", None, "tensor"),
        P("tensor", "dp"),
        P("dp", "tensor", None),
    )
    out_specs = (
        P("dp", "tensor", None),
        P("dp", "tensor", None),
        P(),
        P("dp", None, "tensor", None),
        P("dp", None, "tensor"),
        P(None, None, "tensor", "dp"),
        P(),
        P(),
        P("tensor", "dp"),
        P("dp", None, "tensor"),
        P("tensor", "dp"),
    )
    return jax.shard_map(local, mesh=mesh, in_specs=in_specs, out_specs=out_specs, check_vma=False)
```

time: 1690 us -> 633 us (0.37)
  matrix products: 598 us -> 88.2 us
  local copies, waits for them, and re-layouts: 299 us -> 69.3 us
  other arithmetic: 216 us -> 34.9 us
  blocking collectives: 145 us -> 39 us
  waiting for transfers between devices: 384 us -> 296 us
  Pallas kernels: 0 us -> 69.6 us
  loops' own time: 21.3 us -> 0 us
    dot_general x1061 -> x4, matrix products: 533 us -> 34.7 us  [the longest x1 11.3 us: local(): projected = jnp.dot(normed_all, mix_full, preferred_element_type=f32)]
    all_gather x8 -> x2, waiting for transfers between devices: 214 us -> 84.4 us  [the longest x1 47.6 us: local(): mix_full = lax.all_gather(mixer_pack, 'dp', axis=0, tiled=True)]
    ppermute x0 -> x8, waiting for transfers between devices: none -> 123 us  [swap(): return lax.ppermute(rows, 'tensor', [(0, 1), (1, 0)])]
    squeeze x130 -> x0, local copies, waits for them, and re-layouts: 84.8 us -> none  [the longest x112 81.6 us: delta_rule(): lax.scan(jax.checkpoint(span_step), (memory, no_doc), (to_blocks(queries)...]
    reduce_scatter x8 -> x1, waiting for transfers between devices: 168 us -> 88.1 us  [local(): lax.psum_scatter(jnp.concatenate([up_grad.astype(bf16), down_grad.astype(...]
    pallas_call x0 -> x2, Pallas kernels: none -> 69.6 us  [the longest x1 37.5 us: mixer_backward(): pl.pallas_call(functools.partial(backward_kernel, heads), grid=(count,),...]
    unnamed x1 -> x0, blocking collectives: 62.5 us -> none
    reduce_sum x57 -> x0, other arithmetic: 55.5 us -> none  [the longest x3 28.2 us: short_conv(): weight[tap_count - 1 - offset] * shifted * same_doc[:, None, None]]
  transfers between devices with their start and end apart: 17 -> 12, of which waited for: 11 -> 9; matrix products, arithmetic and copies ran while one was open for 62% -> 16% of each run, Pallas kernels for 0% -> 5%
where the time goes in v1:
time: 633 us; the launch traced here: 623 us
  waiting for transfers between devices  296 us (47%)
  matrix products  88.2 us (14%)
  Pallas kernels  69.6 us (11%)
  local copies, waits for them, and re-layouts  69.3 us (11%)
  blocking collectives  39 us (6%)
  other arithmetic  34.9 us (6%)
  between operations  14.8 us (2%)
  starting transfers between devices  11 us (2%)
    ppermute x8, waiting for transfers between devices, swap(): return lax.ppermute(rows, 'tensor', [(0, 1), (1, 0)])  123 us
    reduce_scatter x1, waiting for transfers between devices, local(): lax.psum_scatter(jnp.concatenate([up_grad.astype(bf16), down_grad.astype(...  88.1 us
    all_gather x1, waiting for transfers between devices, local(): mix_full = lax.all_gather(mixer_pack, 'dp', axis=0, tiled=True)  47.6 us
    psum x1, blocking collectives, local(): small = lax.psum(small, ('dp', 'tensor'))  39 us
    pallas_call x1, Pallas kernels, mixer_backward(): pl.pallas_call(functools.partial(backward_kernel, heads), grid=(count,),...  37.5 us
    all_gather x1, waiting for transfers between devices, local(): rest_full = lax.all_gather(rest_pack, 'dp', axis=0, tiled=True)  36.9 us
    pallas_call x1, Pallas kernels, mixer_forward(): pl.pallas_call(functools.partial(forward_kernel, heads), grid=(count,), i...  32.1 us
    dot_general x4, matrix products, contract_last(): lax.dot_general(operand, other, (((1,), (1,)), ((), ())), preferred_eleme...  27 us
  transfers between devices with their start and end apart: 12, of which 9 were waited for; matrix products, arithmetic and copies ran while one was open for 16% of the time, Pallas kernels for 5%

profile of v1, /device:TPU:0, one launch (start us, length us, event | category | flops | bytes accessed | tf_op | source)
XLA Modules:
  0.0 622.9 jit_solution(9336485777134900314)
XLA Ops:
  18.1 47.6 %all-gather.3.cloned.1.call-done = bf16[1024,2176]{1,0:T(8,128)(2,1)} async-done(((bf16[64,2176]{1,0:T(8,128)(2,1)}), bf16[1024,2176]{1,0:T(8,128)(2,1)}) %all-gather.3.cloned.1.call-update) | async-done | bytes 4456464 | tf_op jit(solution)/shard_map/all_gather | solution.py:525
  66.9 11.3 %fusion.33.proj_ref.before_ref = f32[1024,2176]{1,0:T(8,128)} fusion(bf16[1024,2176]{1,0:T(8,128)(2,1)} %all-gather.3.cloned.1.call-done, bf16[512,1024]{1,0:T(8,128)(2,1)S(1)} %collective-permute-done, bf16[512,1024]{1,0:T(8,128)(2,1)S(1)} %fusion.14, pred[]{:T(512)S(6)} %eq.2), kind=kOutput, calls=%fused_computation.73 | convolution fusion | flops 4572839936 | bytes 15466497 | tf_op jit(solution)/shard_map/dot_general | solution.py:551
  78.4 32.1 %mixer_forward.1 = (bf16[1024,512]{1,0:T(8,128)(2,1)S(1)}, bf16[1024,512]{1,0:T(8,128)(2,1)S(1)}, bf16[1024,512]{1,0:T(8,128)(2,1)S(1)}, bf16[1024,512]{1,0:T(8,...) custom-call(f32[1024,2176]{1,0:T(8,128)} %fusion.33.proj_ref.before_ref, ...), custom_call_target="tpu_custom_call" | custom-call | tf_op jit(solution)/shard_map/mixer_forward/pallas_call | solution.py:378
  113.3 36.9 %all-gather.5.cloned.1.call-done = bf16[1024,4736]{1,0:T(8,128)(2,1)} async-done(((bf16[64,4736]{1,0:T(8,128)(2,1)}), bf16[1024,4736]{1,0:T(8,128)(2,1)}) %all-gather.5.cloned.1.call-update) | async-done | bytes 9699344 | tf_op jit(solution)/shard_map/all_gather | solution.py:529
  154.7 24.2 %collective-permute-done.1 = bf16[512,1024]{1,0:T(8,128)(2,1)S(1)} collective-permute-done((bf16[512,1024]{1,0:T(8,128)(2,1)S(1)}, bf16[512,1024]{1,0:T(8,128)(2,1)S(1)}, u32[]{:S(2)}, u32[]{:S(2)}) %collective-permute-start.1) | collective-permute-done | bytes 1048608 | tf_op jit(solution)/shard_map/ppermute | solution.py:471
  183.0 24.1 %collective-permute-done.2 = bf16[512,1024]{1,0:T(8,128)(2,1)S(1)} collective-permute-done((bf16[512,1024]{1,0:T(8,128)(2,1)S(1)}, bf16[512,1024]{1,0:T(8,128)(2,1)S(1)}, u32[]{:S(2)}, u32[]{:S(2)}) %collective-permute-start.2) | collective-permute-done | bytes 1048608 | tf_op jit(solution)/shard_map/ppermute | solution.py:471
  208.1 9.8 %fusion.6 = f32[1024,2816]{1,0:T(8,128)} fusion(bf16[1024,4736]{1,0:T(8,128)(2,1)S(1)} %bitcast.120, bf16[512,1024]{1,0:T(8,128)(2,1)S(1)} %collective-permute-done.2, bf16[512,1024]{1,0:T(8,128)(2,1)S(1)} %multiply_convert_fusion.1), kind=kOutput, calls=%fused_computation.17 | convolution fusion | flops 5909774336 | bytes 19398656 | tf_op jit(solution)/shard_map/dot_general | solution.py:556
  217.8 14.3 %reshape.136 = f32[1024,2,1408]{2,1,0:T(2,128)} reshape(f32[1024,2816]{1,0:T(8,128)} %fusion.6) | data formatting | bytes 23068672 | tf_op jit(solution)/shard_map/reshape | solution.py:556
  232.1 13.2 %fusion.47 = (f32[1024,1,1408]{2,1,0:T(1,128)S(1)}, f32[1024,1,1408]{2,1,0:T(1,128)}) fusion(f32[1024,2,1408]{2,1,0:T(2,128)} %reshape.136), kind=kLoop, calls=%fused_computation.99 | loop fusion | bytes 23068672 | tf_op jit(solution)/shard_map/jvp()/slice | solution.py:455
  245.4 10.8 %multiply_bitcast_fusion = (f32[1024,1,1408]{2,0,1:T(8,128)S(1)}, f32[1024,1,1408]{2,0,1:T(8,128)}, bf16[1024,1408]{1,0:T(8,128)(2,1)}) fusion(f32[1024,1,1408]{2,1,0:T(1,128)S(1)} %get-tuple-element.75, f32[1024,1,1408]{2,1,0:T(1,128)} %get-tuple-element.76, bf16[1024,4736]{1,0:T(8,128)(2,1)} %all-gather.5.cloned.1.call-done, ...), kind=kOutput, calls=%fused_computation.9 | convolution fusion | flops 2977169408 | bytes 30932992 | tf_op jit(solution)/shard_map/dot_general | solution.py:562
  262.0 8.3 %copy.45 = bf16[1024,2,1408]{0,2,1:T(8,128)(2,1)} copy(bf16[1024,2,1408]{2,0,1:T(8,128)(2,1)} %add_convert_fusion) | data formatting | bytes 11534336 | tf_op jit(solution)/shard_map/convert_element_type | solution.py:565
  270.3 10.2 %fusion.4 = f32[1024,1024]{1,0:T(8,128)S(1)} fusion(bf16[1024,2816]{0,1:T(8,128)(2,1)} %bitcast.95, bf16[1024,4736]{1,0:T(8,128)(2,1)} %all-gather.5.cloned.1.call-done), kind=kOutput, calls=%fused_computation.15 | convolution fusion | flops 5905580032 | bytes 15728640 | tf_op jit(solution)/shard_map/dot_general | solution.py:459
  288.4 18.4 %collective-permute-done.5 = bf16[512,1024]{1,0:T(8,128)(2,1)S(1)} collective-permute-done((bf16[512,1024]{1,0:T(8,128)(2,1)S(1)}, bf16[512,1024]{1,0:T(8,128)(2,1)S(1)}, u32[]{:S(2)}, u32[]{:S(2)}) %collective-permute-start.5) | collective-permute-done | bytes 1048608 | tf_op jit(solution)/shard_map/ppermute | solution.py:471
  307.6 17.7 %collective-permute-done.3 = bf16[512,1024]{1,0:T(8,128)(2,1)S(1)} collective-permute-done((bf16[512,1024]{1,0:T(8,128)(2,1)S(1)}, bf16[512,1024]{1,0:T(8,128)(2,1)S(1)}, u32[]{:S(2)}, u32[]{:S(2)}) %collective-permute-start.3) | collective-permute-done | bytes 1048608 | tf_op jit(solution)/shard_map/ppermute | solution.py:471
  330.3 19.8 %collective-permute-done.6 = bf16[512,1024]{1,0:T(8,128)(2,1)S(1)} collective-permute-done((bf16[512,1024]{1,0:T(8,128)(2,1)S(1)}, bf16[512,1024]{1,0:T(8,128)(2,1)S(1)}, u32[]{:S(2)}, u32[]{:S(2)}) %collective-permute-start.6) | collective-permute-done | bytes 1048608 | tf_op jit(solution)/shard_map/ppermute | solution.py:471
  353.0 37.5 %mixer_backward.1 = (bf16[1024,2176]{1,0:T(8,128)(2,1)}, f32[12,512]{1,0:T(8,128)S(1)}, f32[1,128]{1,0:T(1,128)S(1)}, f32[1,128]{1,0:T(1,128)S(1)}) custom-call(f32[1024,2176]{1,0:T(8,128)} %fusion.33.proj_ref.before_ref, f32[1024,128]{1,0:T(8,128)S(1)} %broadcast_in_dim.36.seg_ref.seg_before_ref, f32[1024,128]{1,0:T(8,128)S(1)} %broadcast_in_dim.36.seg_ref.seg_before_ref, ...), custom_call_target="tpu_custom_call" | custom-call | tf_op jit(solution)/shard_map/mixer_backward/pallas_call | solution.py:417
  390.6 7.6 %fusion.32 = bf16[1024,2176]{0,1:T(8,128)(2,1)S(1)} fusion(bf16[1024,2176]{1,0:T(8,128)(2,1)} %get-tuple-element.27, bf16[512,1024]{1,0:T(8,128)(2,1)S(1)} %copy-done.27, bf16[512,1024]{1,0:T(8,128)(2,1)S(1)} %copy-done.15, pred[]{:T(512)S(6)} %eq.2), kind=kOutput, calls=%fused_computation.72 | convolution fusion | flops 4572839936 | bytes 11010049 | tf_op jit(solution)/shard_map/dot_general | solution.py:465
  404.4 9.8 %pad_maximum_fusion.1 = bf16[1024,2688]{0,1:T(8,128)(2,1)} fusion(bf16[1024,512]{0,1:T(8,128)(2,1)S(1)} %convolution_convert_fusion.2, bf16[1024,48]{0,1:T(8,128)(2,1)S(1)} %copy.50, bf16[1024,2056]{0,1:T(8,128)(2,1)S(1)} %slice-done, bf16[2688]{0:T(1024)(128)(2,1)S(1)} %pad.36.clone), kind=kLoop, calls=%fused_computation.14 | loop fusion | flops 22020096 | bytes 10867968 | tf_op jit(solution)/shard_map/concatenate | solution.py:588
  414.2 8.0 %copy.51 = bf16[1024,2688]{1,0:T(8,128)(2,1)} copy(bf16[1024,2688]{0,1:T(8,128)(2,1)} %pad_maximum_fusion.1) | data formatting | bytes 11010048
  428.4 9.8 %convolution_convert_fusion = bf16[1024,2816]{1,0:T(8,128)(2,1)S(1)} fusion(bf16[1024,2816]{0,1:T(8,128)(2,1)} %bitcast.96, bf16[512,1024]{1,0:T(8,128)(2,1)S(1)} %copy-done.29, bf16[512,1024]{1,0:T(8,128)(2,1)S(1)} %copy-done.17), kind=kOutput, calls=%fused_computation.13 | convolution fusion | flops 5912657920 | bytes 13631488 | tf_op jit(solution)/shard_map/dot_general | solution.py:465
  442.0 8.2 %fusion.53 = f32[1024,1024]{1,0:T(8,128)S(1)} fusion(bf16[1024,2176]{1,0:T(8,128)(2,1)} %get-tuple-element.27, bf16[1024,2176]{1,0:T(8,128)(2,1)} %all-gather.3.cloned.1.call-done), kind=kOutput, calls=%fused_computation.103 | convolution fusion | flops 4563402752 | bytes 13107200 | tf_op jit(solution)/shard_map/dot_general | solution.py:459
  453.8 19.2 %collective-permute-done.7 = bf16[512,1024]{1,0:T(8,128)(2,1)S(1)} collective-permute-done((bf16[512,1024]{1,0:T(8,128)(2,1)S(1)}, bf16[512,1024]{1,0:T(8,128)(2,1)S(1)}, u32[]{:S(2)}, u32[]{:S(2)}) %collective-permute-start.7) | collective-permute-done | bytes 1048608 | tf_op jit(solution)/shard_map/ppermute | solution.py:471
  473.9 39.0 %psum.7 = f32[2184]{0:T(1024)S(1)} all-reduce(f32[2184]{0:T(1024)S(1)} %pad_maximum_fusion.9), channel_id=1, replica_groups=mesh['dp'=16,'tensor'=2] {'dp','tensor'}, use_global_device_ids=true, to_apply=%region_6.7 | all-reduce | flops 2184 | bytes 17472 | tf_op jit(solution)/shard_map/psum | solution.py:610
  523.6 88.1 %reduce-scatter.5.cloned.1.call-done = bf16[64,4224]{1,0:T(8,128)(2,1)} async-done(((bf16[1024,4224]{1,0:T(8,128)(2,1)}), bf16[64,4224]{1,0:T(8,128)(2,1)}) %reduce-scatter.5.cloned.1.call-update) | async-done | bytes 540688 | tf_op jit(solution)/shard_map/reduce_scatter | solution.py:567
  (164 shorter events, 82.2 us)
Async XLA Ops:
  7.2 58.5 %all-gather.3.cloned.1.call-start = ((), (), s32[]{:S(2)}) async-start(), calls=%async_computation.2 | async-start | bytes 4734976 | tf_op jit(solution)/shard_map/all_gather | solution.py:525
  10.9 139.3 %all-gather.5.cloned.1.call-start = ((), (), s32[]{:S(2)}) async-start(), calls=%async_computation.3 | async-start | bytes 10305536 | tf_op jit(solution)/shard_map/all_gather | solution.py:529
  13.8 505.1 %reduce-scatter.7.cloned.1.call-start = ((), (), s32[]{:S(2)}) async-start(), calls=%async_computation.5 | async-start | bytes 5849088
  14.1 64.1 %copy-start.20 = (f32[512]{0:T(512)}, f32[512]{0:T(512)S(1)}, u32[]{:S(2)}) copy-start(f32[512]{0:T(512)S(1)} %fusion.34) | copy-start | bytes 6148
  15.0 63.2 %copy-start.14 = (bf16[512,1024]{1,0:T(8,128)(2,1)}, bf16[512,1024]{1,0:T(8,128)(2,1)S(1)}, u32[]{:S(2)}) copy-start(bf16[512,1024]{1,0:T(8,128)(2,1)S(1)} %fusion.14) | copy-start | bytes 3145732
  15.0 51.9 %collective-permute-start = (bf16[512,1024]{1,0:T(8,128)(2,1)S(1)}, bf16[512,1024]{1,0:T(8,128)(2,1)S(1)}, u32[]{:S(2)}, u32[]{:S(2)}) collective-permute-start(bf16[512,1024]{1,0:T(8,128)(2,1)S(1)} %fusion.14), channel_id=1, source_target_pairs={{0,1},{1,0},{2,3},{3,2},{4,5},{5,4},{6,7},{7,6},{8,9},{9,8},{10,11... | collective-permute-start | bytes 3145736 | tf_op jit(solution)/shard_map/ppermute | solution.py:471
  150.1 28.7 %copy-start.8 = (bf16[1,512,1024]{2,1,0:T(8,128)(2,1)S(1)}, bf16[1,512,1024]{2,1,0:T(8,128)(2,1)}, u32[]{:S(2)}) copy-start(bf16[1,512,1024]{2,1,0:T(8,128)(2,1)} %param.12) | copy-start | bytes 3145732
  150.1 57.9 %slice-start.1 = ((s8[9699328]{0:T(1024)(128)(4,1)}), s8[4194304]{0:T(1024)(128)(4,1)S(1)}, s32[]{:S(2)}) async-start(s8[9699328]{0:T(1024)(128)(4,1)} %bitcast.119), calls=%async_computation.7 | async-start | bytes 8388608
  150.1 57.9 %slice-start.2 = ((s8[9699328]{0:T(1024)(128)(4,1)}), s8[4194304]{0:T(1024)(128)(4,1)S(1)}, s32[]{:S(2)}) async-start(s8[9699328]{0:T(1024)(128)(4,1)} %bitcast.119), calls=%async_computation.8 | async-start | bytes 8388608
  153.5 54.6 %slice-start.3 = ((s8[9699328]{0:T(1024)(128)(4,1)}), s8[1310720]{0:T(1024)(128)(4,1)S(1)}, s32[]{:S(2)}) async-start(s8[9699328]{0:T(1024)(128)(4,1)} %bitcast.119), calls=%async_computation.9 | async-start | bytes 2621440
  153.5 25.4 %collective-permute-start.1 = (bf16[512,1024]{1,0:T(8,128)(2,1)S(1)}, bf16[512,1024]{1,0:T(8,128)(2,1)S(1)}, u32[]{:S(2)}, u32[]{:S(2)}) collective-permute-start(bf16[512,1024]{1,0:T(8,128)(2,1)S(1)} %slice.211), channel_id=1, source_target_pairs={{0,1},{1,0},{2,3},{3,2},{4,5},{5,4},{6,7},{7,6},{8,9},{9,8},{10,11... | collective-permute-start | bytes 3145736 | tf_op jit(solution)/shard_map/ppermute | solution.py:471
  180.9 26.2 %copy-start.16 = (bf16[512,1024]{1,0:T(8,128)(2,1)}, bf16[512,1024]{1,0:T(8,128)(2,1)S(1)}, u32[]{:S(2)}) copy-start(bf16[512,1024]{1,0:T(8,128)(2,1)S(1)} %multiply_convert_fusion.1) | copy-start | bytes 3145732
  180.9 26.2 %collective-permute-start.2 = (bf16[512,1024]{1,0:T(8,128)(2,1)S(1)}, bf16[512,1024]{1,0:T(8,128)(2,1)S(1)}, u32[]{:S(2)}, u32[]{:S(2)}) collective-permute-start(bf16[512,1024]{1,0:T(8,128)(2,1)S(1)} %multiply_convert_fusion.1), channel_id=1, source_target_pairs={{0,1},{1,0},{2,3},{3,2},{4,5},{5,4},{6,7},{7,6},{8,9},{9,8},{10,11... | collective-permute-start | bytes 3145736 | tf_op jit(solution)/shard_map/ppermute | solution.py:471
  182.1 63.3 %collective-permute-start.4 = (bf16[512,1024]{1,0:T(8,128)(2,1)}, bf16[512,1024]{1,0:T(8,128)(2,1)}, u32[]{:S(2)}, u32[]{:S(2)}) collective-permute-start(bf16[512,1024]{1,0:T(8,128)(2,1)} %bitcast.18), channel_id=1, source_target_pairs={{0,1},{1,0},{2,3},{3,2},{4,5},{5,4},{6,7},{7,6},{8,9},{9,8},{10,11... | collective-permute-start | bytes 3145736 | tf_op jit(solution)/shard_map/ppermute | solution.py:471
  280.7 26.2 %collective-permute-start.5 = (bf16[512,1024]{1,0:T(8,128)(2,1)S(1)}, bf16[512,1024]{1,0:T(8,128)(2,1)S(1)}, u32[]{:S(2)}, u32[]{:S(2)}) collective-permute-start(bf16[512,1024]{1,0:T(8,128)(2,1)S(1)} %slice.209), channel_id=1, source_target_pairs={{0,1},{1,0},{2,3},{3,2},{4,5},{5,4},{6,7},{7,6},{8,9},{9,8},{10,11... | collective-permute-start | bytes 3145736 | tf_op jit(solution)/shard_map/ppermute | solution.py:471
  281.9 24.9 %copy-start.6 = (f32[512,1024]{1,0:T(8,128)S(1)}, f32[512,1024]{1,0:T(8,128)}, u32[]{:S(2)}) copy-start(f32[512,1024]{1,0:T(8,128)} %copy-done.5) | copy-start | bytes 6291460
  287.5 37.7 %collective-permute-start.3 = (bf16[512,1024]{1,0:T(8,128)(2,1)S(1)}, bf16[512,1024]{1,0:T(8,128)(2,1)S(1)}, u32[]{:S(2)}, u32[]{:S(2)}) collective-permute-start(bf16[512,1024]{1,0:T(8,128)(2,1)S(1)} %slice.210), channel_id=1, source_target_pairs={{0,1},{1,0},{2,3},{3,2},{4,5},{5,4},{6,7},{7,6},{8,9},{9,8},{10,11... | collective-permute-start | bytes 3145736 | tf_op jit(solution)/shard_map/ppermute | solution.py:471
  329.0 24.0 %copy-start.12 = (bf16[512,1024]{1,0:T(8,128)(2,1)}, bf16[512,1024]{1,0:T(8,128)(2,1)S(1)}, u32[]{:S(2)}) copy-start(bf16[512,1024]{1,0:T(8,128)(2,1)S(1)} %get-tuple-element.68) | copy-start | bytes 3145732
  329.0 21.1 %collective-permute-start.6 = (bf16[512,1024]{1,0:T(8,128)(2,1)S(1)}, bf16[512,1024]{1,0:T(8,128)(2,1)S(1)}, u32[]{:S(2)}, u32[]{:S(2)}) collective-permute-start(bf16[512,1024]{1,0:T(8,128)(2,1)S(1)} %get-tuple-element.68), channel_id=1, source_target_pairs={{0,1},{1,0},{2,3},{3,2},{4,5},{5,4},{6,7},{7,6},{8,9},{9,8},{10,11... | collective-permute-start | bytes 3145736 | tf_op jit(solution)/shard_map/ppermute | solution.py:471
  353.0 37.6 %copy-start.15 = (bf16[512,1024]{1,0:T(8,128)(2,1)S(1)}, bf16[512,1024]{1,0:T(8,128)(2,1)}, u32[]{:S(2)}) copy-start(bf16[512,1024]{1,0:T(8,128)(2,1)} %copy-done.14) | copy-start | bytes 3145732
  353.0 37.6 %copy-start.27 = (bf16[512,1024]{1,0:T(8,128)(2,1)S(1)}, bf16[512,1024]{1,0:T(8,128)(2,1)}, u32[]{:S(2)}) copy-start(bf16[512,1024]{1,0:T(8,128)(2,1)} %copy-done.26) | copy-start | bytes 3145732
  422.3 189.4 %reduce-scatter.5.cloned.1.call-start = ((), (), s32[]{:S(2)}) async-start(), calls=%async_computation.4 | async-start | bytes 9191424 | tf_op jit(solution)/shard_map/reduce_scatter | solution.py:567
  452.2 62.3 %copy-start.23 = (f32[512]{0:T(512)S(1)}, f32[512]{0:T(512)}, u32[]{:S(2)}) copy-start(f32[512]{0:T(512)} %copy-done.22) | copy-start | bytes 6148
  452.4 20.5 %collective-permute-start.7 = (bf16[512,1024]{1,0:T(8,128)(2,1)S(1)}, bf16[512,1024]{1,0:T(8,128)(2,1)S(1)}, u32[]{:S(2)}, u32[]{:S(2)}) collective-permute-start(bf16[512,1024]{1,0:T(8,128)(2,1)S(1)} %slice.208), channel_id=1, source_target_pairs={{0,1},{1,0},{2,3},{3,2},{4,5},{5,4},{6,7},{7,6},{8,9},{9,8},{10,11... | collective-permute-start | bytes 3145736 | tf_op jit(solution)/shard_map/ppermute | solution.py:471
  (25 other events, 211.2 us)
Sparse Core Ops, SparseCore 0:
  11.0 54.6 all-gather.2
  68.5 81.5 all-gather.4
  422.4 78.3 reduce-scatter.6
  505.2 106.4 reduce-scatter.4

commit v2 on v1

--- a/solution.py
+++ b/solution.py
@@ -10,6 +10,7 @@
 CHUNK = 128
 WIDTH = 128
 HALO = 8
+COLUMN_TILE = 256
 norm_eps = 1e-05
 unit_eps = 1e-06
 f32 = jnp.float32
@@ -439,6 +440,209 @@
     )(proj, seg_wide, seg_wide, proj, conv_rows, neg_rate, gain, grad, *saved)
 
 
+def project_kernel(x_ref, w_ref, out_ref):
+    out_ref[...] = dot(x_ref[...], w_ref[...], NN)
+
+
+def project(x, packed, columns):
+    rows, model = x.shape
+    return pl.pallas_call(
+        project_kernel,
+        grid=(pl.cdiv(columns, COLUMN_TILE),),
+        in_specs=[
+            pl.BlockSpec((rows, model), lambda i: (0, 0)),
+            pl.BlockSpec((model, COLUMN_TILE), lambda i: (0, i)),
+        ],
+        out_specs=pl.BlockSpec((rows, COLUMN_TILE), lambda i: (0, i)),
+        out_shape=jax.ShapeDtypeStruct((rows, columns), f32),
+        compiler_params=pltpu.CompilerParams(vmem_limit_bytes=40 * 1024 * 1024),
+        cost_estimate=pl.CostEstimate(
+            flops=2 * rows * model * columns,
+            bytes_accessed=2 * model * (rows + columns) + 4 * rows * columns,
+            transcendentals=0,
+        ),
+        name="project",
+    )(x, packed)
+
+
+def ffn_kernel(tiles, x_ref, dy_ref, w_ref, h_ref, g_ref, y_ref, dx_ref, y_sum, dx_sum):
+    step = pl.program_id(0)
+
+    @pl.when(step == 0)
+    def _():
+        y_sum[...] = jnp.zeros_like(y_sum)
+        dx_sum[...] = jnp.zeros_like(dx_sum)
+
+    def units(size):
+        gate_up = dot(x_ref[...], w_ref[:, : 2 * size], NN)
+        grad = dot(dy_ref[...], w_ref[:, 2 * size : 3 * size], NN)
+        gate, up = gate_up[:, :size], gate_up[:, size:]
+        gate_s = sigmoid(gate)
+        act = gate * gate_s
+        h_ref[:, :size] = (act * up).astype(bf16)
+        g_ref[:, :size] = (grad * up * (gate_s + act * (1.0 - gate_s))).astype(bf16)
+        g_ref[:, size : 2 * size] = (grad * act).astype(bf16)
+        y_sum[...] += dot(h_ref[:, :size], w_ref[:, 2 * size : 3 * size], NT)
+        dx_sum[...] += dot(g_ref[:, : 2 * size], w_ref[:, : 2 * size], NT)
+
+    per_tile(tiles, step, units)
+
+    @pl.when(step == len(tiles) - 1)
+    def _():
+        y_ref[...] = y_sum[...].astype(bf16)
+        dx_ref[...] = dx_sum[...].astype(bf16)
+
+
+def per_tile(tiles, step, units):
+    if tiles[0] == tiles[-1]:
+        units(tiles[0])
+        return
+
+    @pl.when(step < len(tiles) - 1)
+    def _():
+        units(tiles[0])
+
+    @pl.when(step == len(tiles) - 1)
+    def _():
+        units(tiles[-1])
+
+
+def ffn(x, dy, packed, tiles):
+    rows, model = x.shape
+    hidden = sum(tiles)
+    whole = pl.BlockSpec((rows, model), lambda i: (0, 0))
+    return pl.pallas_call(
+        functools.partial(ffn_kernel, tiles),
+        grid=(len(tiles),),
+        in_specs=[whole, whole, pl.BlockSpec((model, 3 * tiles[0]), lambda i: (0, i))],
+        out_specs=[
+            pl.BlockSpec((rows, tiles[0]), lambda i: (0, i)),
+            pl.BlockSpec((rows, 2 * tiles[0]), lambda i: (0, i)),
+            whole,
+            whole,
+        ],
+        out_shape=[
+            jax.ShapeDtypeStruct((rows, hidden), bf16),
+            jax.ShapeDtypeStruct((rows, 2 * hidden), bf16),
+            jax.ShapeDtypeStruct((rows, model), bf16),
+            jax.ShapeDtypeStruct((rows, model), bf16),
+        ],
+        scratch_shapes=[pltpu.VMEM((rows, model), f32), pltpu.VMEM((rows, model), f32)],
+        compiler_params=pltpu.CompilerParams(vmem_limit_bytes=48 * 1024 * 1024),
+        cost_estimate=pl.CostEstimate(
+            flops=12 * rows * model * hidden,
+            bytes_accessed=2 * (3 * model * hidden + rows * (4 * model + 3 * hidden)),
+            transcendentals=rows * hidden,
+        ),
+        name="ffn",
+    )(x, dy, packed)
+
+
+def ffn_grads_kernel(tiles, *refs):
+    *inputs, out_ref, x_turned, dy_turned = refs
+    xs, dys, hs, gs = (inputs[at : at + len(inputs) // 4] for at in range(0, len(inputs), len(inputs) // 4))
+    step = pl.program_id(0)
+    rows = xs[0].shape[0]
+
+    @pl.when(step == 0)
+    def _():
+        for at, (x_ref, dy_ref) in enumerate(zip(xs, dys)):
+            x_turned[:, at * rows : (at + 1) * rows] = x_ref[...].T
+            dy_turned[:, at * rows : (at + 1) * rows] = dy_ref[...].T
+
+    def units(size):
+        up_grad, down_grad = None, None
+        for at, (h_ref, g_ref) in enumerate(zip(hs, gs)):
+            lanes = slice(at * rows, (at + 1) * rows)
+            up_term = dot(x_turned[:, lanes], g_ref[:, : 2 * size], NN)
+            down_term = dot(dy_turned[:, lanes], h_ref[:, :size], NN)
+            up_grad = up_term if at == 0 else up_grad + up_term
+            down_grad = down_term if at == 0 else down_grad + down_term
+        out_ref[:, : 2 * size] = up_grad.astype(bf16)
+        out_ref[:, 2 * size : 3 * size] = down_grad.astype(bf16)
+
+    per_tile(tiles, step, units)
+
+
+def ffn_grads(xs, dys, hs, gs, tiles):
+    rows, model = xs[0].shape
+    hidden = sum(tiles)
+    whole = pl.BlockSpec((rows, model), lambda i: (0, 0))
+    total = rows * len(xs)
+    return pl.pallas_call(
+        functools.partial(ffn_grads_kernel, tiles),
+        grid=(len(tiles),),
+        in_specs=[whole] * (2 * len(xs))
+        + [pl.BlockSpec((rows, tiles[0]), lambda i: (0, i))] * len(xs)
+        + [pl.BlockSpec((rows, 2 * tiles[0]), lambda i: (0, i))] * len(xs),
+        out_specs=pl.BlockSpec((model, 3 * tiles[0]), lambda i: (0, i)),
+        out_shape=jax.ShapeDtypeStruct((model, 3 * hidden), bf16),
+        scratch_shapes=[pltpu.VMEM((model, total), bf16), pltpu.VMEM((model, total), bf16)],
+        compiler_params=pltpu.CompilerParams(vmem_limit_bytes=48 * 1024 * 1024),
+        cost_estimate=pl.CostEstimate(
+            flops=6 * total * model * hidden,
+            bytes_accessed=2 * (3 * model * hidden + total * (2 * model + 3 * hidden)),
+            transcendentals=0,
+        ),
+        name="ffn_grads",
+    )(*xs, *dys, *hs, *gs)
+
+
+def mixer_grads_kernel(
+    tile, main_steps, normed_ref, residual_ref, dproj_ref, mixed_ref, conv_ref, out_ref, turned
+):
+    step = pl.program_id(0)
+    last = pl.num_programs(0) - 1
+
+    @pl.when(step == 0)
+    def _():
+        turned[...] = normed_ref[...].T
+
+    @pl.when(step < main_steps)
+    def _():
+        out_ref[...] = dot(turned[...], dproj_ref[...], NN).astype(bf16)
+
+    @pl.when((step >= main_steps) & (step < last))
+    def _():
+        out_ref[...] = dot(residual_ref[...], mixed_ref[...], TN).astype(bf16)
+
+    @pl.when(step == last)
+    def _():
+        grads = dot(turned[...], dproj_ref[:, :WIDTH], NN) + conv_ref[...]
+        out_ref[:, :WIDTH] = grads.astype(bf16)
+
+
+def mixer_grads(normed, residual, dproj, mixed, conv_block):
+    rows, model = normed.shape
+    wide = mixed.shape[1]
+    tile = 2 * WIDTH if wide % (2 * WIDTH) == 0 else WIDTH
+    main_steps = 4 * wide // tile
+    out_steps = wide // tile
+    columns = 5 * wide + WIDTH
+    whole = pl.BlockSpec((rows, model), lambda i: (0, 0))
+    return pl.pallas_call(
+        functools.partial(mixer_grads_kernel, tile, main_steps),
+        grid=(main_steps + out_steps + 1,),
+        in_specs=[
+            whole,
+            whole,
+            pl.BlockSpec((rows, tile), lambda i: (0, jnp.minimum(i, main_steps))),
+            pl.BlockSpec((rows, tile), lambda i: (0, jnp.clip(i - main_steps, 0, out_steps - 1))),
+            pl.BlockSpec((model, WIDTH), lambda i: (0, 0)),
+        ],
+        out_specs=pl.BlockSpec((model, tile), lambda i: (0, i)),
+        out_shape=jax.ShapeDtypeStruct((model, columns), bf16),
+        scratch_shapes=[pltpu.VMEM((model, rows), bf16)],
+        compiler_params=pltpu.CompilerParams(vmem_limit_bytes=40 * 1024 * 1024),
+        cost_estimate=pl.CostEstimate(
+            flops=2 * rows * model * columns,
+            bytes_accessed=2 * (2 * rows * model + (rows + model) * columns),
+            transcendentals=0,
+        ),
+        name="mixer_grads",
+    )(normed, residual, dproj, mixed, conv_block)
+
+
 def rms_norm(values, scales):
     return values * lax.rsqrt(jnp.mean(values * values, axis=-1, keepdims=True) + norm_eps) * scales
 
@@ -449,10 +653,6 @@
 
 def second_norm(values, gains):
     return rms_norm(values, gains[1])
-
-
-def swish_product(gate_up):
-    return jax.nn.silu(gate_up[:, 0]) * gate_up[:, 1]
 
 
 def contract_last(operand, other):
@@ -469,6 +669,67 @@
 
 def swap(rows):
     return lax.ppermute(rows, "tensor", [(0, 1), (1, 0)])
+
+
+def sum_over(values, axis):
+    size = lax.axis_size(axis)
+    if size & (size - 1):
+        return lax.psum(values, axis)
+    bit = 1
+    while bit < size:
+        values = values + lax.ppermute(values, axis, [(i, i ^ bit) for i in range(size)])
+        bit *= 2
+    return values
+
+
+def hidden_tiles(hidden):
+    if hidden % WIDTH:
+        return (hidden,)
+    return (2 * WIDTH,) * (hidden // (2 * WIDTH)) + (WIDTH,) * (hidden // WIDTH % 2)
+
+
+def pack_tiles(gate, up, down, tiles):
+    blocks = []
+    at = 0
+    for size in tiles:
+        blocks += [part[:, at : at + size] for part in (gate, up, down)]
+        at += size
+    return jnp.concatenate(blocks, axis=1)
+
+
+def unpack_tiles(packed, tiles):
+    parts = ([], [], [])
+    at = 0
+    for size in tiles:
+        for part in parts:
+            part.append(packed[:, at : at + size])
+            at += size
+    return [jnp.concatenate(part, axis=1) for part in parts]
+
+
+def ffn_plain(x, dy, packed, tiles):
+    gate_w, up_w, down_w = unpack_tiles(packed, tiles)
+    gate = jnp.dot(x, gate_w, preferred_element_type=f32)
+    up = jnp.dot(x, up_w, preferred_element_type=f32)
+    grad = jnp.dot(dy, down_w, preferred_element_type=f32)
+    gate_s = sigmoid(gate)
+    act = gate * gate_s
+    hidden = (act * up).astype(bf16)
+    gate_grad = (grad * up * (gate_s + act * (1.0 - gate_s))).astype(bf16)
+    up_grad = (grad * act).astype(bf16)
+    share = contract_last(hidden, down_w).astype(bf16)
+    dx = (contract_last(gate_grad, gate_w) + contract_last(up_grad, up_w)).astype(bf16)
+    return hidden, jnp.concatenate([gate_grad, up_grad], axis=1), share, dx
+
+
+def ffn_grads_plain(x, dy, hidden, grads, tiles):
+    size = hidden.shape[1]
+    return pack_tiles(
+        contract_first(x, grads[:, :size]).astype(bf16),
+        contract_first(x, grads[:, size:]).astype(bf16),
+        contract_first(dy, hidden).astype(bf16),
+        tiles,
+    )
 
 
 def local(
@@ -486,50 +747,50 @@
     cotangent,
 ):
     dp_size = lax.axis_size("dp")
-    tensor_size = lax.axis_size("tensor")
+    pair = lax.axis_size("tensor") == 2
     tensor_rank = lax.axis_index("tensor")
     rows_here, _, heads, _ = w_mixer_in.shape
     model_width = rows_here * dp_size
     wide = heads * WIDTH
     hidden_here = w_gate_up.shape[2]
+    tiles = hidden_tiles(hidden_here)
+    kernels = hidden_here % WIDTH == 0
     taps_here = conv_weight.shape[3]
-    conv_at = 4 * wide + 2 * heads
-    out_here = w_output.shape[0]
     own_rows = tokens.shape[1]
+    projected_width = 4 * wide + WIDTH
 
     def gather_rows(rows):
-        if tensor_size == 2:
-            return jnp.concatenate([rows, swap(rows)], axis=0)
         return lax.all_gather(rows, "tensor", axis=0, tiled=True)
 
-    def sum_rows(product):
-        if tensor_size == 2:
-            return product[:own_rows] + swap(product[own_rows:].astype(bf16)).astype(f32)
-        return lax.psum_scatter(
-            product.astype(bf16), "tensor", scatter_dimension=0, tiled=True
-        ).astype(f32)
-
-    def in_order(rows):
-        if tensor_size == 2:
-            turned = jnp.concatenate([rows[own_rows:], rows[:own_rows]], axis=0)
-            return jnp.where(tensor_rank == 0, rows, turned)
-        return rows
+    def scatter_rows(product):
+        return lax.psum_scatter(product.astype(bf16), "tensor", scatter_dimension=0, tiled=True)
+
+    def in_order(own, other):
+        first = tensor_rank == 0
+        return jnp.concatenate([jnp.where(first, own, other), jnp.where(first, other, own)], axis=0)
+
+    def own_and_other(rows):
+        own = lax.dynamic_slice_in_dim(rows, tensor_rank * own_rows, own_rows)
+        return own, lax.dynamic_slice_in_dim(rows, (1 - tensor_rank) * own_rows, own_rows)
 
     conv_block = jnp.pad(
         conv_weight.transpose(3, 0, 1, 2).reshape(taps_here, 12 * heads),
         ((0, rows_here - taps_here), (0, WIDTH - 14 * heads)),
     )
     mixer_pack = jnp.concatenate(
-        [w_mixer_in.reshape(rows_here, -1), w_rates.reshape(rows_here, -1), conv_block], axis=1
+        [
+            w_mixer_in.reshape(rows_here, -1),
+            w_rates.reshape(rows_here, -1),
+            conv_block,
+            w_output.T,
+        ],
+        axis=1,
     )
     mix_full = lax.all_gather(mixer_pack, "dp", axis=0, tiled=True)
-    rest_pack = jnp.concatenate(
-        [w_gate_up.reshape(rows_here, -1), w_output.T, w_down.T], axis=1
-    )
-    rest_full = lax.all_gather(rest_pack, "dp", axis=0, tiled=True)
-    up_full = rest_full[:, : 2 * hidden_here]
-    out_full = rest_full[:, 2 * hidden_here : 2 * hidden_here + out_here]
-    down_full = rest_full[:, 2 * hidden_here + out_here :]
+    ffn_pack = pack_tiles(w_gate_up[:, 0], w_gate_up[:, 1], w_down.T, tiles)
+    ffn_full = lax.all_gather(ffn_pack, "dp", axis=0, tiled=True)
+    out_mine = mix_full[:, projected_width:]
+    conv_at = 4 * wide + 2 * heads
     conv_rows = (
         mix_full[:, conv_at : conv_at + 12 * heads]
         .reshape(dp_size, rows_here, 12 * heads)[:, :taps_here]
@@ -543,87 +804,108 @@
     )[None]
     gain_row = out_gain[None]
 
-    grad_local = cotangent[0]
-    grad_all = gather_rows(grad_local)
+    grad_own = cotangent[0]
     inputs = tokens[0].astype(f32)
     normed, first_back = jax.vjp(first_norm, inputs, norm_gains)
-    normed_all = in_order(gather_rows(normed.astype(bf16)))
-    projected = jnp.dot(normed_all, mix_full, preferred_element_type=f32)
+    normed = normed.astype(bf16)
+    if pair:
+        normed_all = in_order(normed, swap(normed))
+        grad_other = swap(grad_own)
+        out_other = swap(out_mine)
+    else:
+        normed_all = gather_rows(normed)
+    projected = project(normed_all, mix_full, projected_width)
     mixed, *saved = mixer_forward(projected, segment, conv_rows, neg_rate, gain_row)
-    residual = inputs + sum_rows(contract_last(in_order(mixed), out_full))
+    if pair:
+        mixed_own, mixed_theirs = own_and_other(mixed)
+        share = contract_last(mixed_own, out_mine) + contract_last(swap(mixed_theirs), out_other)
+    else:
+        share = scatter_rows(contract_last(mixed, out_mine)).astype(f32)
+    residual = inputs + share
     normed_ffn, second_back = jax.vjp(second_norm, residual, norm_gains)
-    ffn_all = gather_rows(normed_ffn.astype(bf16))
-    gate_up = jnp.dot(ffn_all, up_full, preferred_element_type=f32).reshape(-1, 2, hidden_here)
-    hidden_raw, swish_back = jax.vjp(swish_product, gate_up)
-    hidden = hidden_raw.astype(bf16)
-    result = residual + sum_rows(contract_last(hidden, down_full))
-    out_tokens = result.astype(bf16)[None]
-
-    hidden_grad = jnp.dot(grad_all, down_full, preferred_element_type=f32)
-    down_grad = contract_first(grad_all, hidden)
-    (gate_up_grad,) = swish_back(hidden_grad)
-    gate_up_low = gate_up_grad.reshape(-1, 2 * hidden_here).astype(bf16)
-    up_grad = contract_first(ffn_all, gate_up_low)
-    rest_grads = lax.psum_scatter(
-        jnp.concatenate([up_grad.astype(bf16), down_grad.astype(bf16)], axis=1),
-        "dp",
-        scatter_dimension=0,
-        tiled=True,
-    )
-    ffn_input_grad = sum_rows(contract_last(gate_up_low, up_full))
-    residual_part, second_gains = second_back(ffn_input_grad)
-    residual_grad = grad_local.astype(f32) + residual_part
-    residual_all = in_order(gather_rows(residual_grad.astype(bf16)))
-    mixed_grad = jnp.dot(residual_all, out_full, preferred_element_type=f32)
-    out_grad = contract_first(residual_all, mixed)
+    normed_ffn = normed_ffn.astype(bf16)
+    if pair:
+        x_both = [normed_ffn, swap(normed_ffn)]
+        dy_both = [grad_own, grad_other]
+    else:
+        x_both = [gather_rows(normed_ffn)]
+        dy_both = [gather_rows(grad_own)]
+    one_ffn = ffn if kernels else ffn_plain
+    done = [one_ffn(x, dy, ffn_full, tiles) for x, dy in zip(x_both, dy_both)]
+    h_both, g_both, y_both, dx_both = zip(*done)
+    if pair:
+        dx = dx_both[0].astype(f32) + swap(dx_both[1]).astype(f32)
+        y_other = swap(y_both[1])
+        y = y_both[0].astype(f32) + y_other.astype(f32)
+    else:
+        dx = scatter_rows(dx_both[0]).astype(f32)
+        y = scatter_rows(y_both[0]).astype(f32)
+    out_tokens = (residual + y).astype(bf16)[None]
+    if kernels:
+        ffn_sums = ffn_grads(x_both, dy_both, h_both, g_both, tiles)
+    else:
+        ffn_sums = ffn_grads_plain(x_both[0], dy_both[0], h_both[0], g_both[0], tiles)
+    residual_part, second_gains = second_back(dx)
+    residual_grad = grad_own.astype(f32) + residual_part
+    residual_low = residual_grad.astype(bf16)
+    if pair:
+        grad_theirs = jnp.dot(residual_low, out_other, preferred_element_type=f32).astype(bf16)
+        grad_mine = jnp.dot(residual_low, out_mine, preferred_element_type=f32).astype(bf16)
+        mixed_grad = in_order(grad_mine, swap(grad_theirs))
+    else:
+        residual_all = gather_rows(residual_low)
+        mixed_grad = jnp.dot(residual_all, out_mine, preferred_element_type=f32).astype(bf16)
+    mixed_grad, ffn_sums = lax.optimization_barrier((mixed_grad, ffn_sums))
+    ffn_owned = lax.psum_scatter(ffn_sums, "dp", scatter_dimension=0, tiled=True)
+    if pair:
+        residual_all = in_order(residual_low, swap(residual_low))
     projection_grad, conv_grad, log_grad, gain_grad = mixer_backward(
         projected, segment, conv_rows, neg_rate, gain_row, mixed_grad, saved
     )
-    mix_grad = contract_first(normed_all, projection_grad)
     conv_grad = jnp.pad(
         conv_grad.reshape(12 * heads, WIDTH).T.reshape(dp_size, taps_here, 12 * heads),
-        ((0, 0), (0, rows_here - taps_here), (0, 0)),
-    ).reshape(model_width, 12 * heads)
-    mix_grads = lax.psum_scatter(
-        jnp.concatenate(
-            [
-                mix_grad[:, :conv_at].astype(bf16),
-                conv_grad.astype(bf16),
-                jnp.zeros((model_width, WIDTH - 14 * heads), bf16),
-                out_grad.astype(bf16),
-            ],
-            axis=1,
-        ),
-        "dp",
-        scatter_dimension=0,
-        tiled=True,
-    ).astype(f32)
-    mixer_input_grad = sum_rows(in_order(contract_last(projection_grad, mix_full)))
+        ((0, 0), (0, rows_here - taps_here), (2 * heads, WIDTH - 14 * heads)),
+    ).reshape(model_width, WIDTH)
+    mix_sums = mixer_grads(normed_all, residual_all, projection_grad, mixed, conv_grad)
+    mix_sums, projection_grad = lax.optimization_barrier((mix_sums, projection_grad))
+    mix_owned = lax.psum_scatter(mix_sums, "dp", scatter_dimension=0, tiled=True).astype(f32)
+    mix_rows = mix_full[:, :projected_width]
+    if pair:
+        grad_here, grad_there = own_and_other(projection_grad)
+        mixer_input_grad = swap(contract_last(grad_there, mix_rows).astype(bf16)).astype(f32)
+        mixer_input_grad = mixer_input_grad + contract_last(grad_here, mix_rows)
+    else:
+        mixer_input_grad = scatter_rows(contract_last(projection_grad, mix_rows)).astype(f32)
     input_part, first_gains = first_back(mixer_input_grad)
     input_grad = (residual_grad + input_part).astype(bf16)[None]
     log_full = lax.dynamic_update_slice_in_dim(
         jnp.zeros(a_log.shape, f32), log_grad[0, :heads], tensor_rank * heads, 0
     )
     small = jnp.concatenate(
-        [(first_gains + second_gains).reshape(-1), gain_grad.reshape(-1), log_full]
-    )
-    small = lax.psum(small, ("dp", "tensor"))
-    gain_count = 2 * model_width
-    rest_grads = rest_grads.astype(f32)
+        [
+            (first_gains + second_gains).reshape(-1, WIDTH),
+            gain_grad,
+            jnp.pad(log_full, (0, WIDTH - log_full.shape[0]))[None],
+        ]
+    )
+    small = sum_over(sum_over(small, "dp"), "tensor")
+    gain_rows = 2 * model_width // WIDTH
+    gate_grad, up_grad, down_grad = unpack_tiles(ffn_owned, tiles)
+    rates = mix_owned[:, 5 * wide :]
     return (
         out_tokens,
         input_grad,
-        small[:gain_count].reshape(2, model_width),
-        mix_grads[:, : 4 * wide].reshape(w_mixer_in.shape),
-        mix_grads[:, 4 * wide : conv_at].reshape(w_rates.shape),
-        mix_grads[:taps_here, conv_at : conv_at + 12 * heads]
+        small[:gain_rows].reshape(2, model_width),
+        mix_owned[:, : 4 * wide].reshape(w_mixer_in.shape),
+        rates[:, : 2 * heads].reshape(w_rates.shape),
+        rates[:taps_here, 2 * heads : 14 * heads]
         .reshape(taps_here, 3, 4, heads)
         .transpose(1, 2, 3, 0),
-        small[gain_count + WIDTH :],
-        small[gain_count : gain_count + WIDTH],
-        mix_grads[:, 4 * wide + WIDTH :].T,
-        rest_grads[:, : 2 * hidden_here].reshape(w_gate_up.shape),
-        rest_grads[:, 2 * hidden_here :].T,
+        small[gain_rows + 1, : a_log.shape[0]],
+        small[gain_rows],
+        mix_owned[:, 4 * wide : 5 * wide].T,
+        jnp.stack([gate_grad, up_grad], axis=1).astype(f32),
+        down_grad.T.astype(f32),
     )
 
 

time: 633 us -> 523 us (0.83); the launches traced: 623 us -> 522 us
  matrix products: 88.2 us -> 23.2 us
  Pallas kernels: 69.6 us -> 131 us
  blocking collectives: 39 us -> 0 us
  local copies, waits for them, and re-layouts: 69.3 us -> 36.4 us
  other arithmetic: 34.9 us -> 13.4 us
  waiting for transfers between devices: 296 us -> 288 us
    pallas_call x0 -> x5, Pallas kernels: none -> 62.3 us  [the longest x2 28.2 us: ffn(): pl.pallas_call(functools.partial(ffn_kernel, tiles), grid=(len(tiles),),...]
    dot_general x8 -> x2, matrix products: 61.2 us -> 5.52 us  [the longest x1 3.04 us: local(): jnp.dot(residual_low, out_other, preferred_element_type=f32).astype(bf16)]
    psum x1 -> x0, blocking collectives: 39 us -> none  [local(): small = lax.psum(small, ('dp', 'tensor'))]
    all_gather x1, waiting for transfers between devices: 36.9 us -> 0.01 us  [local(): ffn_full = lax.all_gather(ffn_pack, 'dp', axis=0, tiled=True)]
    reduce_scatter x1 -> x2, waiting for transfers between devices: 88.1 us -> 122 us  [the longest x1 106 us: local(): lax.psum_scatter(ffn_sums, 'dp', scatter_dimension=0, tiled=True)]
    all_gather x1, waiting for transfers between devices: 47.6 us -> 29.8 us  [local(): mix_full = lax.all_gather(mixer_pack, 'dp', axis=0, tiled=True)]
    concatenate x4, other arithmetic: 15.4 us -> 0.43 us  [the longest x3 0.42 us: in_order(): jnp.concatenate([jnp.where(first, own, other), jnp.where(first, other, ow...]
    reshape x3 -> x4, local copies, waits for them, and re-layouts: 16.2 us -> 2.54 us  [the longest x1 1.14 us: local(): mix_owned[:, :4 * wide].reshape(w_mixer_in.shape)]
  transfers between devices with their start and end apart: 12 -> 19, of which waited for: 9 -> 14; matrix products, arithmetic and copies ran while one was open for 16% -> 8% of each run, Pallas kernels for 5% -> 20%
where the time goes in v2:
time: 523 us; the launch traced here: 522 us
  waiting for transfers between devices  288 us (55%)
  Pallas kernels  131 us (25%)
  local copies, waits for them, and re-layouts  36.4 us (7%)
  matrix products  23.2 us (4%)
  starting transfers between devices  14.8 us (3%)
  between operations  14.4 us (3%)
  other arithmetic  13.4 us (3%)
    ppermute x10, waiting for transfers between devices, swap(): return lax.ppermute(rows, 'tensor', [(0, 1), (1, 0)])  123 us
    reduce_scatter x1, waiting for transfers between devices, local(): lax.psum_scatter(ffn_sums, 'dp', scatter_dimension=0, tiled=True)  106 us
    pallas_call x1, Pallas kernels, mixer_backward(): pl.pallas_call(functools.partial(backward_kernel, heads), grid=(count,),...  36.9 us
    pallas_call x1, Pallas kernels, mixer_forward(): pl.pallas_call(functools.partial(forward_kernel, heads), grid=(count,), i...  32.1 us
    all_gather x1, waiting for transfers between devices, local(): mix_full = lax.all_gather(mixer_pack, 'dp', axis=0, tiled=True)  29.8 us
    pallas_call x2, Pallas kernels, ffn(): pl.pallas_call(functools.partial(ffn_kernel, tiles), grid=(len(tiles),),...  28.2 us
    unnamed x95, local copies, waits for them, and re-layouts  19.9 us
    dot_general x4, matrix products, contract_last(): lax.dot_general(operand, other, (((1,), (1,)), ((), ())), preferred_eleme...  17.7 us
  transfers between devices with their start and end apart: 19, of which 14 were waited for; matrix products, arithmetic and copies ran while one was open for 8% of the time, Pallas kernels for 20%

profile of v2, /device:TPU:0, one launch (start us, length us, event | category | flops | bytes accessed | tf_op | source)
XLA Modules:
  0.0 521.6 jit_solution(8451350881117550965)
XLA Ops:
  18.1 23.3 %collective-permute-done = bf16[512,1024]{1,0:T(8,128)(2,1)S(1)} collective-permute-done((bf16[512,1024]{1,0:T(8,128)(2,1)}, bf16[512,1024]{1,0:T(8,128)(2,1)S(1)}, u32[]{:S(2)}, u32[]{:S(2)}) %collective-permute-start) | collective-permute-done | bytes 1048608 | tf_op jit(solution)/shard_map/ppermute | solution.py:671
  42.1 29.8 %all-gather.3.cloned.1.call-done.w_ref = bf16[1024,2688]{1,0:T(8,128)(2,1)} async-done(((bf16[64,2688]{1,0:T(8,128)(2,1)}), bf16[1024,2688]{1,0:T(8,128)(2,1)}) %all-gather.3.cloned.1.call-update) | async-done | bytes 5505040 | tf_op jit(solution)/shard_map/all_gather | solution.py:789
  79.4 9.0 %project.1.proj_ref.before_ref = f32[1024,2176]{1,0:T(8,128)} custom-call(bf16[1024,1024]{1,0:T(8,128)(2,1)S(1)} %pad_maximum_fusion.x_ref.normed_ref, bf16[1024,2688]{1,0:T(8,128)(2,1)S(1)} %copy-done.15), custom_call_target="tpu_custom_call" | custom-call | flops 4563402752 | bytes 15466496 | tf_op jit(solution)/shard_map/project/pallas_call | solution.py:449
  88.6 32.1 %mixer_forward.1 = (bf16[1024,512]{1,0:T(8,128)(2,1)S(1)}, bf16[1024,512]{1,0:T(8,128)(2,1)S(1)}, bf16[1024,512]{1,0:T(8,128)(2,1)S(1)}, bf16[1024,512]{1,0:T(8,...) custom-call(f32[1024,2176]{1,0:T(8,128)} %project.1.proj_ref.before_ref, ...), custom_call_target="tpu_custom_call" | custom-call | tf_op jit(solution)/shard_map/mixer_forward/pallas_call | solution.py:379
  128.6 10.9 %collective-permute-done.1 = bf16[512,512]{1,0:T(8,128)(2,1)S(1)} collective-permute-done((bf16[512,512]{1,0:T(8,128)(2,1)}, bf16[512,512]{1,0:T(8,128)(2,1)S(1)}, u32[]{:S(2)}, u32[]{:S(2)}) %collective-permute-start.1) | collective-permute-done | bytes 524320 | tf_op jit(solution)/shard_map/ppermute | solution.py:671
  143.6 18.5 %collective-permute-done.4.dy_ref.refs_3_ = bf16[512,1024]{1,0:T(8,128)(2,1)} collective-permute-done((bf16[512,1024]{1,0:T(8,128)(2,1)S(1)}, bf16[512,1024]{1,0:T(8,128)(2,1)}, u32[]{:S(2)}, u32[]{:S(2)}) %collective-permute-start.4) | collective-permute-done | bytes 1048608 | tf_op jit(solution)/shard_map/ppermute | solution.py:671
  162.1 21.4 %collective-permute-done.3.x_ref.refs_1_ = bf16[512,1024]{1,0:T(8,128)(2,1)S(1)} collective-permute-done((bf16[512,1024]{1,0:T(8,128)(2,1)S(1)}, bf16[512,1024]{1,0:T(8,128)(2,1)S(1)}, u32[]{:S(2)}, u32[]{:S(2)}) %collective-permute-start.3) | collective-permute-done | bytes 1048608 | tf_op jit(solution)/shard_map/ppermute | solution.py:671
  185.7 14.4 %ffn.3 = (bf16[512,1408]{1,0:T(8,128)(2,1)S(1)}, bf16[512,2816]{1,0:T(8,128)(2,1)}, bf16[512,1024]{1,0:T(8,128)(2,1)}, bf16[512,1024]{1,0:T(8,128)(2,1)S(1)}) custom-call(bf16[512,1024]{1,0:T(8,128)(2,1)S(1)} %copy-done.19, bf16[512,1024]{1,0:T(8,128)(2,1)} %collective-permute-done.4.dy_ref.refs_3_, bf16[1024,4224]{1,0:T(8,128)(2,1)} %all-gather.5.cloned.1.call-done.w_ref), custom_call_target="tpu_custom_call" | custom-call | flops 8858370048 | bytes 17170432 | tf_op jit(solution)/shard_map/ffn/pallas_call | solution.py:514
  201.8 13.8 %ffn.2 = (bf16[512,1408]{1,0:T(8,128)(2,1)S(1)}, bf16[512,2816]{1,0:T(8,128)(2,1)}, bf16[512,1024]{1,0:T(8,128)(2,1)S(1)}, bf16[512,1024]{1,0:T(8,128)(2,1)S(1)}) custom-call(bf16[512,1024]{1,0:T(8,128)(2,1)S(1)} %copy-done.4, bf16[512,1024]{1,0:T(8,128)(2,1)S(1)} %bitcast.73, bf16[1024,4224]{1,0:T(8,128)(2,1)} %all-gather.5.cloned.1.call-done.w_ref), custom_call_target="tpu_custom_call" | custom-call | flops 8858370048 | bytes 17170432 | tf_op jit(solution)/shard_map/ffn/pallas_call | solution.py:514
  215.6 9.8 %collective-permute-done.6 = bf16[512,1024]{1,0:T(8,128)(2,1)S(1)} collective-permute-done((bf16[512,1024]{1,0:T(8,128)(2,1)S(1)}, bf16[512,1024]{1,0:T(8,128)(2,1)S(1)}, u32[]{:S(2)}, u32[]{:S(2)}) %collective-permute-start.6) | collective-permute-done | bytes 1048608 | tf_op jit(solution)/shard_map/ppermute | solution.py:671
  228.7 3.0 convolution_convert_fusion
  233.2 14.6 %ffn_grads.1 = bf16[1024,4224]{1,0:T(8,128)(2,1)} custom-call(bf16[512,1024]{1,0:T(8,128)(2,1)S(1)} %copy-done.4, bf16[512,1024]{1,0:T(8,128)(2,1)S(1)} %copy-done.20, bf16[512,1024]{1,0:T(8,128)(2,1)S(1)} %bitcast.74, bf16[512,1024]{1,0:T(8,128)(2,1)} %collective-permute-done.4.dy_ref.refs_3_, bf16[512,1408]{1,0:T(8,128)(2,1)S(1)} %get-tuple-element.38.refs_4_, ...), custom_call_target="tpu_custom_call" | custom-call | flops 8858370048 | bytes 21495808 | tf_op jit(solution)/shard_map/ffn_grads/pallas_call | solution.py:572
  247.9 15.1 %collective-permute-done.8 = bf16[512,512]{1,0:T(8,128)(2,1)} collective-permute-done((bf16[512,512]{1,0:T(8,128)(2,1)}, bf16[512,512]{1,0:T(8,128)(2,1)}, u32[]{:S(2)}, u32[]{:S(2)}) %collective-permute-start.8) | collective-permute-done | bytes 524320 | tf_op jit(solution)/shard_map/ppermute | solution.py:671
  267.0 36.9 %mixer_backward.1 = (bf16[1024,2176]{1,0:T(8,128)(2,1)}, f32[12,512]{1,0:T(8,128)S(1)}, f32[1,128]{1,0:T(1,128)S(1)}, f32[1,128]{1,0:T(1,128)S(1)}) custom-call(f32[1024,2176]{1,0:T(8,128)} %project.1.proj_ref.before_ref, f32[1024,128]{1,0:T(8,128)S(1)} %broadcast_in_dim.30.seg_ref.seg_before_ref, f32[1024,128]{1,0:T(8,128)S(1)} %broadcast_in_dim.30.seg_ref.seg_before_ref, ...), custom_call_target="tpu_custom_call" | custom-call | tf_op jit(solution)/shard_map/mixer_backward/pallas_call | solution.py:418
  308.1 10.6 %mixer_grads.1 = bf16[1024,2688]{1,0:T(8,128)(2,1)} custom-call(bf16[1024,1024]{1,0:T(8,128)(2,1)S(1)} %copy-done.2, bf16[1024,1024]{1,0:T(8,128)(2,1)S(1)} %pad_maximum_fusion.1.residual_ref, bf16[1024,2176]{1,0:T(8,128)(2,1)S(1)} %copy-done.17, bf16[1024,512]{1,0:T(8,128)(2,1)S(1)} %copy-done.6, f32[1024,128]{1,0:T(8,128)S(1)} %bitcast.75), custom_call_target="tpu_custom_call" | custom-call | flops 5637144576 | bytes 15204352 | tf_op jit(solution)/shard_map/mixer_grads/pallas_call | solution.py:623
  319.3 5.8 %fusion.16 = bf16[512,1024]{1,0:T(8,128)(2,1)S(1)} fusion(bf16[1024,2688]{1,0:T(8,128)(2,1)} %all-gather.3.cloned.1.call-done.w_ref, bf16[1024,2176]{1,0:T(8,128)(2,1)} %get-tuple-element.50.dproj_ref, s32[]{:T(128)S(6)} %select_n.49), kind=kOutput, calls=%fused_computation.32 | convolution fusion | flops 2282225664 | bytes 7733252 | tf_op jit(solution)/shard_map/dot_general | solution.py:659
  327.3 24.0 %collective-permute-done.9 = bf16[512,1024]{1,0:T(8,128)(2,1)S(1)} collective-permute-done((bf16[512,1024]{1,0:T(8,128)(2,1)S(1)}, bf16[512,1024]{1,0:T(8,128)(2,1)S(1)}, u32[]{:S(2)}, u32[]{:S(2)}) %collective-permute-start.9) | collective-permute-done | bytes 1048608 | tf_op jit(solution)/shard_map/ppermute | solution.py:671
  351.3 7.6 %fusion.9 = (f32[1024]{0:T(1024)S(1)}, f32[512]{0:T(512)S(1)}, f32[512,1024]{1,0:T(8,128)}) fusion(bf16[1,512,1024]{2,1,0:T(8,128)(2,1)S(1)} %copy-done.26, f32[512]{0:T(512)S(1)} %fusion.25, bf16[512,1024]{1,0:T(8,128)(2,1)S(1)} %collective-permute-done.9, f32[1024]{0:T(1024)S(1)} %bitcast.95, bf16[1024,2688]{1,0:T(8,128)(2,1)} %all-gather.3.cloned.1.call-done.w_ref, ...), kind=kOutput, calls=%fused_computation.16 | convolution fusion | flops 2286418432 | bytes 10891268 | tf_op jit(solution)/shard_map/dot_general | solution.py:659
  360.7 3.4 collective-permute-done.11
  365.4 3.2 collective-permute-done.12
  369.7 5.0 collective-permute-done.13
  374.7 5.3 %fusion.22 = (bf16[1,512,1024]{2,1,0:T(8,128)(2,1)}, bf16[1,512,1024]{2,1,0:T(8,128)(2,1)}) fusion(bf16[1,512,1024]{2,1,0:T(8,128)(2,1)} %param.12, f32[512]{0:T(512)S(1)} %multiply_multiply_fusion, f32[1024]{0:T(1024)S(1)} %bitcast.96, f32[512]{0:T(512)S(1)} %fusion.25, f32[512,1024]{1,0:T(8,128)} %get-tuple-element.113, bf16[512,1024]{1,0:T(8,128)(2,1)} %copy-done.30, ...), kind=kLoop, calls=%fused_computation.36 | loop fusion | flops 13107200 | bytes 13647872 | tf_op jit(solution)/shard_map/broadcast_in_dim | solution.py:880
  381.6 15.7 %reduce-scatter.3.cloned.1.call-done = bf16[64,2688]{1,0:T(8,128)(2,1)} async-done(((bf16[1024,2688]{1,0:T(8,128)(2,1)}), bf16[64,2688]{1,0:T(8,128)(2,1)}) %reduce-scatter.3.cloned.1.call-update) | async-done | bytes 344080 | tf_op jit(solution)/shard_map/reduce_scatter | solution.py:871
  401.7 106.4 %reduce-scatter.5.cloned.1.call-done = bf16[64,4224]{1,0:T(8,128)(2,1)} async-done(((bf16[1024,4224]{1,0:T(8,128)(2,1)}), bf16[64,4224]{1,0:T(8,128)(2,1)}) %reduce-scatter.5.cloned.1.call-update) | async-done | bytes 540688 | tf_op jit(solution)/shard_map/reduce_scatter | solution.py:859
  (189 shorter events, 67.7 us)
Async XLA Ops:
  7.2 64.7 %all-gather.3.cloned.1.call-start = ((), (), s32[]{:S(2)}) async-start(), calls=%async_computation.2 | async-start | bytes 5849088 | tf_op jit(solution)/shard_map/all_gather | solution.py:789
  11.7 172.8 %all-gather.5.cloned.1.call-start = ((), (), s32[]{:S(2)}) async-start(), calls=%async_computation.3 | async-start | bytes 9191424 | tf_op jit(solution)/shard_map/all_gather | solution.py:791
  13.4 383.9 %reduce-scatter.3.cloned.1.call-start = ((), (), s32[]{:S(2)}) async-start(), calls=%async_computation.4 | async-start | bytes 5849088 | tf_op jit(solution)/shard_map/reduce_scatter | solution.py:871
  15.1 26.3 %collective-permute-start = (bf16[512,1024]{1,0:T(8,128)(2,1)}, bf16[512,1024]{1,0:T(8,128)(2,1)S(1)}, u32[]{:S(2)}, u32[]{:S(2)}) collective-permute-start(bf16[512,1024]{1,0:T(8,128)(2,1)} %fusion.8), channel_id=1, source_target_pairs={{0,1},{1,0},{2,3},{3,2},{4,5},{5,4},{6,7},{7,6},{8,9},{9,8},{10,11... | collective-permute-start | bytes 3145736 | tf_op jit(solution)/shard_map/ppermute | solution.py:671
  42.1 46.3 %copy-start.1 = (bf16[1024,1024]{1,0:T(8,128)(2,1)}, bf16[1024,1024]{1,0:T(8,128)(2,1)S(1)}, u32[]{:S(2)}) copy-start(bf16[1024,1024]{1,0:T(8,128)(2,1)S(1)} %pad_maximum_fusion.x_ref.normed_ref) | copy-start | bytes 6291460
  75.4 64.2 %collective-permute-start.2 = (bf16[1024,512]{1,0:T(8,128)(2,1)}, bf16[1024,512]{1,0:T(8,128)(2,1)}, u32[]{:S(2)}, u32[]{:S(2)}) collective-permute-start(bf16[1024,512]{1,0:T(8,128)(2,1)} %slice.213), channel_id=1, source_target_pairs={{0,1},{1,0},{2,3},{3,2},{4,5},{5,4},{6,7},{7,6},{8,9},{9,8},{10,11... | collective-permute-start | bytes 3145736 | tf_op jit(solution)/shard_map/ppermute | solution.py:671
  88.6 36.5 %copy-start = (bf16[1,512,1024]{2,1,0:T(8,128)(2,1)S(1)}, bf16[1,512,1024]{2,1,0:T(8,128)(2,1)}, u32[]{:S(2)}) copy-start(bf16[1,512,1024]{2,1,0:T(8,128)(2,1)} %param.23) | copy-start | bytes 3145732
  124.5 15.0 %collective-permute-start.1 = (bf16[512,512]{1,0:T(8,128)(2,1)}, bf16[512,512]{1,0:T(8,128)(2,1)S(1)}, u32[]{:S(2)}, u32[]{:S(2)}) collective-permute-start(bf16[512,512]{1,0:T(8,128)(2,1)} %constant_dynamic-slice_fusion), channel_id=1, source_target_pairs={{0,1},{1,0},{2,3},{3,2},{4,5},{5,4},{6,7},{7,6},{8,9},{9,8},{10,11... | collective-permute-start | bytes 1572872 | tf_op jit(solution)/shard_map/ppermute | solution.py:671
  125.1 37.0 %collective-permute-start.4 = (bf16[512,1024]{1,0:T(8,128)(2,1)S(1)}, bf16[512,1024]{1,0:T(8,128)(2,1)}, u32[]{:S(2)}, u32[]{:S(2)}) collective-permute-start(bf16[512,1024]{1,0:T(8,128)(2,1)S(1)} %bitcast.72), channel_id=1, source_target_pairs={{0,1},{1,0},{2,3},{3,2},{4,5},{5,4},{6,7},{7,6},{8,9},{9,8},{10,11... | collective-permute-start | bytes 3145736 | tf_op jit(solution)/shard_map/ppermute | solution.py:671
  142.0 41.5 %collective-permute-start.3 = (bf16[512,1024]{1,0:T(8,128)(2,1)S(1)}, bf16[512,1024]{1,0:T(8,128)(2,1)S(1)}, u32[]{:S(2)}, u32[]{:S(2)}) collective-permute-start(bf16[512,1024]{1,0:T(8,128)(2,1)S(1)} %multiply_convert_fusion.x_ref.refs_0_), channel_id=1, source_target_pairs={{0,1},{1,0},{2,3},{3,2},{4,5},{5,4},{6,7},{7,6},{8,9},{9,8},{10,11... | collective-permute-start | bytes 3145736 | tf_op jit(solution)/shard_map/ppermute | solution.py:671
  201.2 24.2 %copy-start.23 = (f32[512,1024]{1,0:T(8,128)S(1)}, f32[512,1024]{1,0:T(8,128)}, u32[]{:S(2)}) copy-start(f32[512,1024]{1,0:T(8,128)} %copy-done.22) | copy-start | bytes 6291460
  201.2 24.2 %collective-permute-start.6 = (bf16[512,1024]{1,0:T(8,128)(2,1)S(1)}, bf16[512,1024]{1,0:T(8,128)(2,1)S(1)}, u32[]{:S(2)}, u32[]{:S(2)}) collective-permute-start(bf16[512,1024]{1,0:T(8,128)(2,1)S(1)} %get-tuple-element.37), channel_id=1, source_target_pairs={{0,1},{1,0},{2,3},{3,2},{4,5},{5,4},{6,7},{7,6},{8,9},{9,8},{10,11... | collective-permute-start | bytes 3145736 | tf_op jit(solution)/shard_map/ppermute | solution.py:671
  228.2 75.9 %collective-permute-start.7 = (bf16[512,1024]{1,0:T(8,128)(2,1)}, bf16[512,1024]{1,0:T(8,128)(2,1)}, u32[]{:S(2)}, u32[]{:S(2)}) collective-permute-start(bf16[512,1024]{1,0:T(8,128)(2,1)} %fusion.33), channel_id=1, source_target_pairs={{0,1},{1,0},{2,3},{3,2},{4,5},{5,4},{6,7},{7,6},{8,9},{9,8},{10,11... | collective-permute-start | bytes 3145736 | tf_op jit(solution)/shard_map/ppermute | solution.py:671
  231.8 31.2 %collective-permute-start.8 = (bf16[512,512]{1,0:T(8,128)(2,1)}, bf16[512,512]{1,0:T(8,128)(2,1)}, u32[]{:S(2)}, u32[]{:S(2)}) collective-permute-start(bf16[512,512]{1,0:T(8,128)(2,1)} %convolution_convert_fusion), channel_id=1, source_target_pairs={{0,1},{1,0},{2,3},{3,2},{4,5},{5,4},{6,7},{7,6},{8,9},{9,8},{10,11... | collective-permute-start | bytes 1572872 | tf_op jit(solution)/shard_map/ppermute | solution.py:671
  318.7 189.3 %reduce-scatter.5.cloned.1.call-start = ((), (), s32[]{:S(2)}) async-start(), calls=%async_computation.5 | async-start | bytes 9191424 | tf_op jit(solution)/shard_map/reduce_scatter | solution.py:859
  319.3 32.0 %copy-start.26 = (bf16[1,512,1024]{2,1,0:T(8,128)(2,1)S(1)}, bf16[1,512,1024]{2,1,0:T(8,128)(2,1)}, u32[]{:S(2)}) copy-start(bf16[1,512,1024]{2,1,0:T(8,128)(2,1)} %param.12) | copy-start | bytes 3145732
  325.2 26.2 %collective-permute-start.9 = (bf16[512,1024]{1,0:T(8,128)(2,1)S(1)}, bf16[512,1024]{1,0:T(8,128)(2,1)S(1)}, u32[]{:S(2)}, u32[]{:S(2)}) collective-permute-start(bf16[512,1024]{1,0:T(8,128)(2,1)S(1)} %fusion.16), channel_id=1, source_target_pairs={{0,1},{1,0},{2,3},{3,2},{4,5},{5,4},{6,7},{7,6},{8,9},{9,8},{10,11... | collective-permute-start | bytes 3145736 | tf_op jit(solution)/shard_map/ppermute | solution.py:671
  325.6 49.1 %collective-permute-start.5 = (bf16[512,1024]{1,0:T(8,128)(2,1)}, bf16[512,1024]{1,0:T(8,128)(2,1)}, u32[]{:S(2)}, u32[]{:S(2)}) collective-permute-start(bf16[512,1024]{1,0:T(8,128)(2,1)} %get-tuple-element.35), channel_id=1, source_target_pairs={{0,1},{1,0},{2,3},{3,2},{4,5},{5,4},{6,7},{7,6},{8,9},{9,8},{10,11... | collective-permute-start | bytes 3145736 | tf_op jit(solution)/shard_map/ppermute | solution.py:671
  327.3 47.3 %copy-start.8 = (bf16[512,1024]{1,0:T(8,128)(2,1)S(1)}, bf16[512,1024]{1,0:T(8,128)(2,1)}, u32[]{:S(2)}) copy-start(bf16[512,1024]{1,0:T(8,128)(2,1)} %copy-done.7) | copy-start | bytes 3145732
  359.0 1.2 collective-permute-start.10
  360.3 3.8 collective-permute-start.11
  364.0 4.5 collective-permute-start.12
  368.6 6.1 %collective-permute-start.13 = (f32[18,128]{1,0:T(8,128)S(1)}, f32[18,128]{1,0:T(8,128)S(1)}, u32[]{:S(2)}, u32[]{:S(2)}) collective-permute-start(f32[18,128]{1,0:T(8,128)S(1)} %add.106), channel_id=1, source_target_pairs={{0,16},{2,18},{4,20},{6,22},{8,24},{10,26},{12,28},{14,30},{16,0},... | collective-permute-start | bytes 27656 | tf_op jit(solution)/shard_map/ppermute | solution.py:680
  374.7 5.3 %collective-permute-start.14 = (f32[18,128]{1,0:T(8,128)S(1)}, f32[18,128]{1,0:T(8,128)S(1)}, u32[]{:S(2)}, u32[]{:S(2)}) collective-permute-start(f32[18,128]{1,0:T(8,128)S(1)} %add.107), channel_id=1, source_target_pairs={{0,1},{1,0},{2,3},{3,2},{4,5},{5,4},{6,7},{7,6},{8,9},{9,8},{10,11... | collective-permute-start | bytes 27656 | tf_op jit(solution)/shard_map/ppermute | solution.py:680
  (31 other events, 137.3 us)
Sparse Core Ops, SparseCore 0:
  11.8 60.0 all-gather.2
  74.8 75.1 all-gather.4
  318.8 78.4 reduce-scatter.2
  401.8 106.2 reduce-scatter.4
